TPU v7x, 256 devices: a whole 4x4x8 slice. The times are simulated.
256 devices in a mesh: lon: 64 (over z, y_hi, x), lat: 4 (over y_lo, core).
Axes of the slice: x: 4, y: 4 (y_hi: 2, y_lo: 2; y = y_hi * 2 + y_lo), z: 8, core: 2. Of those that a mesh axis runs over, the one named last changes fastest.
Arguments:
- saved_states: float32 [4, 12, 2048, 2048], P(None, None, 'lon', 'lat'), may hold values from -2 to 2, as said below
- final_cotangent: float32 [12, 2048, 2048], P(None, 'lon', 'lat'), may hold values from -6 to 6
- gravities: float32 [4], replicated, may hold values from 0.3 to 1.5
- sea_mask: int32 [2048, 2048], P('lon', 'lat'), may hold values 0 or 1
- layer_index: int32 [2048, 2048], P('lon', 'lat'), may hold values from 0 to 3
Outputs:
- initial_gradient: float32 [12, 2048, 2048], P(None, 'lon', 'lat')
- forcing_gradient: float32 [2048, 2048], P('lon', 'lat')
Inputs may be any that keep to these rules, and one draw needn't show every extreme that they name: `saved_states`: in each saved state the first 4 channels are layer thicknesses, all positive; the others are velocities.
All inputs are finite; a program needn't handle non-finite values. No bound on the sum of `sea_mask` on one device may be relied on, other than what follows from the above.
Results may differ from a plain program's by a relative error of at most 0.0001.
Values sent between devices are 32-bit elements; how exact they have to be, the bound alone decides.
No kernel may reach another device: no remote copies, remote signals or barrier semaphores. Data moves between devices by JAX's collectives and lax.ppermute only.
A program may use at most 128 MiB of HBM per device.

v0:
```python
import functools

import jax
import jax.numpy as jnp
from jax import lax
from jax.experimental import pallas as pl
from jax.experimental.pallas import tpu as pltpu
from jax.sharding import PartitionSpec as P

TIME_STEP = 0.3
VISCOSITY = 0.1
DIFFUSION = 0.05
BOTTOM_DRAG = 0.2

L = 4
N = 4
CH = 3 * L
ROWS = 32
COLS = 512
RR = ROWS + 2 * N
CC = COLS + 128
T = RR // 8
W = CC // 128


def lanes(j):
    return slice(128 * j, 128 * j + 128)


COT = N * CH
SEA = COT + CH
PLANES = SEA + 1
GROUPS = -(-PLANES // 16)


def depth(q):
    if q >= COT:
        return N
    n, c = divmod(q, CH)
    return n + 1 if c >= L else n


ORDER = sorted(range(PLANES), key=lambda q: -depth(q))
OFFSET = {}
_row = 0
for _q in ORDER:
    if depth(_q):
        OFFSET[_q] = _row
        _row += depth(_q)
HALO_ROWS = _row


def pack_kernel(states, cot, sea, east, west, strips, east_corner, west_corner):
    lane = lax.broadcasted_iota(jnp.int32, (ROWS, 128), 1)

    def plane(q, rows, cols):
        if q == SEA:
            return sea[rows, cols].astype(jnp.float32)
        if q >= COT:
            return cot[q - COT, rows, cols]
        return states[q // CH, q % CH, rows, cols]

    everything = slice(None)
    for q, row in OFFSET.items():
        d = depth(q)
        east[row : row + d] = plane(q, slice(ROWS - d, ROWS), everything)
        west[row : row + d] = plane(q, slice(0, d), everything)
    for g in range(GROUPS):
        total = jnp.zeros((ROWS, 128), jnp.float32)
        for k in range(16):
            q = g * 16 + k
            if q >= PLANES:
                continue
            first = plane(q, everything, slice(0, 128))
            last = plane(q, everything, slice(COLS - 128, COLS))
            both = pltpu.roll(jnp.where(lane >= 124, last, first), (8 * k + 4) % 128, 1)
            total = jnp.where(lane // 8 == k, both, total)
        strips[g] = total
        east_corner[4 * g : 4 * g + 4] = total[ROWS - 4 :]
        west_corner[4 * g : 4 * g + 4] = total[:4]


def step_kernel(
    place,
    gravities,
    states,
    cot,
    sea,
    layer,
    spin,
    from_west,
    from_east,
    from_south,
    from_north,
    sw,
    nw,
    se,
    ne,
    out,
    forcing,
    planes,
    cur,
    nxt,
    mixed,
    acc,
    picked,
    sems,
):
    copies = []
    for n in range(N, -1, -1):
        source = cot if n == N else states.at[n]
        for j in range(W - 1):
            copies.append(
                pltpu.make_async_copy(
                    source.at[:, :, lanes(j)],
                    planes.at[n * CH : (n + 1) * CH, j, :ROWS, :],
                    sems.at[n * W + j],
                )
            )
    for copy in copies:
        copy.start()
    for j in range(W - 1):
        planes[SEA, j, :ROWS, :] = sea[:, lanes(j)].astype(jnp.float32)
        picked[j, :ROWS, :] = layer[:, lanes(j)]

    for q, row in OFFSET.items():
        d = depth(q)
        for j in range(W - 1):
            planes[q, j, ROWS : ROWS + d, :] = from_east[row : row + d, lanes(j)]
            planes[q, j, RR - d : RR, :] = from_west[row : row + d, lanes(j)]
    lane = lax.broadcasted_iota(jnp.int32, (ROWS, 128), 1)
    south_side = lane % 8 < 4
    for g in range(GROUPS):
        edge = jnp.where(south_side, from_south[g], from_north[g])
        rows = slice(4 * g, 4 * g + 4)
        corner = jnp.concatenate(
            [
                jnp.where(south_side[:4], se[rows], ne[rows]),
                jnp.where(south_side[:4], sw[rows], nw[rows]),
            ],
            axis=0,
        )
        for k in range(16):
            q = g * 16 + k
            if q >= PLANES:
                continue
            shift = (128 - (8 * k + 4)) % 128
            planes[q, W - 1, :ROWS, :] = pltpu.roll(edge, shift, 1)
            planes[q, W - 1, ROWS:, :] = pltpu.roll(corner, shift, 1)
    for copy in copies:
        copy.wait()

    def ring(t):
        return pl.ds(t, 8, stride=T)

    def read(q, t):
        return jnp.concatenate([planes[q, j, ring(t), :] for j in range(W)], axis=1)

    def write(q, t, value):
        for j in range(W - 1):
            planes[q, j, ring(t), :] = value[:, lanes(j)]

    for t in range(T):
        sea_t = read(SEA, t)
        for c in range(CH):
            value = read(COT + c, t)
            cur[c, t] = value if c < L else value * sea_t
        acc[t] = jnp.zeros((8, CC), jnp.float32)

    edge_lane = lax.broadcasted_iota(jnp.int32, (8, 128), 1)
    inside = jnp.where(edge_lane < 64, place[0], place[1]) > 0

    def north(x):
        return pltpu.roll(x, CC - 1, 1)

    def south(x):
        return pltpu.roll(x, 1, 1)

    def one_step(index, src, dst):
        n = N - 1 - index

        def east(load, t):
            return load(t + 1) if t + 1 < T else pltpu.roll(load(0), 7, 0)

        def west(load, t):
            return load(t - 1) if t > 0 else pltpu.roll(load(T - 1), 1, 0)

        def layer_body(k, carry):
            load_h = lambda t: read(n * CH + k, t)
            load_u = lambda t: read(n * CH + L + k, t)
            load_v = lambda t: read(n * CH + 2 * L + k, t)
            load_c = lambda t: src[k, t]
            load_p = lambda t: src[L + k, t]
            load_q = lambda t: src[2 * L + k, t]
            half = 0.5 * TIME_STEP
            drag = jnp.where(k == L - 1, BOTTOM_DRAG, 0.0)
            keep = 1.0 - TIME_STEP * (4.0 * VISCOSITY + drag)
            turn = spin[...]
            for t in range(T):
                c, p, q = load_c(t), load_p(t), load_q(t)
                h, u, v = load_h(t), load_u(t), load_v(t)
                ce, cw, cn, cs = east(load_c, t), west(load_c, t), north(c), south(c)
                dcx = ce - cw
                dcy = cn - cs
                pe, pw, pn, ps = east(load_p, t), west(load_p, t), north(p), south(p)
                qe, qw, qn, qs = east(load_q, t), west(load_q, t), north(q), south(q)
                mixed[k, t] = (pe - pw) + (qn - qs)
                dst[k, t] = (1.0 - 4.0 * TIME_STEP * DIFFUSION) * c + half * (
                    u * dcx + v * dcy + (2.0 * DIFFUSION) * ((ce + cw) + (cn + cs))
                )
                ue, uw, un, us = east(load_u, t), west(load_u, t), north(u), south(u)
                ve, vw, vn, vs = east(load_v, t), west(load_v, t), north(v), south(v)
                a_e = ue + 2.0 * VISCOSITY
                a_w = 2.0 * VISCOSITY - uw
                a_n = vn + 2.0 * VISCOSITY
                a_s = 2.0 * VISCOSITY - vs
                new_p = keep * p + half * (
                    h * dcx
                    - turn * q
                    - p * (ue - uw)
                    - q * (ve - vw)
                    + (a_e * pe + a_w * pw)
                    + (a_n * pn + a_s * ps)
                )
                new_q = keep * q + half * (
                    h * dcy
                    + turn * p
                    - p * (un - us)
                    - q * (vn - vs)
                    + (a_e * qe + a_w * qw)
                    + (a_n * qn + a_s * qs)
                )
                mask = jnp.where(n == 0, 1.0, read(SEA, t))
                dst[L + k, t] = new_p * mask
                dst[2 * L + k, t] = new_q * mask
            return carry

        lax.fori_loop(0, L, layer_body, 0)
        half = 0.5 * TIME_STEP
        for t in range(T):
            idx = jnp.concatenate([picked[j, ring(t), :] for j in range(W)], axis=1)
            chosen = jnp.zeros((8, CC), jnp.float32)
            for k in range(L):
                chosen = jnp.where(idx == k, src[k, t], chosen)
            acc[t] = acc[t] + TIME_STEP * chosen
            tails = [None] * L
            total = mixed[L - 1, t]
            tails[L - 1] = total
            for k in range(L - 2, -1, -1):
                total = total + mixed[k, t]
                tails[k] = total
            head = None
            for k in range(L):
                term = (half * gravities[k]) * tails[k]
                head = term if head is None else head + term
                new = dst[k, t] + head
                dst[k, t, :, :COLS] = new[:, :COLS]
                dst[k, t, :, COLS:] = jnp.where(inside, new[:, COLS:], 0.0)

    def two_steps(i, carry):
        one_step(2 * i, cur, nxt)
        one_step(2 * i + 1, nxt, cur)
        return carry

    lax.fori_loop(0, N // 2, two_steps, 0)

    for t in range(T):
        for c in range(CH):
            write(COT + c, t, cur[c, t])
        write(SEA, t, acc[t])
    final = []
    for j in range(W - 1):
        final.append(
            pltpu.make_async_copy(planes.at[COT : COT + CH, j, :ROWS, :], out.at[:, :, lanes(j)], sems.at[2 * j])
        )
        final.append(pltpu.make_async_copy(planes.at[SEA, j, :ROWS, :], forcing.at[:, lanes(j)], sems.at[2 * j + 1]))
    for copy in final:
        copy.start()
    for copy in final:
        copy.wait()


VMEM = pl.BlockSpec(memory_space=pltpu.VMEM)
SMEM = pl.BlockSpec(memory_space=pltpu.SMEM)
ANY = pl.BlockSpec(memory_space=pl.ANY)
f32 = jnp.float32


def per_device(saved_states, final_cotangent, gravities, sea_mask, layer_index):
    lons, lats = lax.axis_size("lon"), lax.axis_size("lat")
    lat = lax.axis_index("lat")
    lane = jnp.arange(CC, dtype=jnp.int32)
    lane = jnp.where(lane < COLS + 64, lane, lane - CC)
    lat_rows = (lat * COLS + lane).astype(f32)
    spin = 2.0 * jnp.sin(jnp.pi * ((lat_rows + 0.5) / (lats * COLS) - 0.5))
    spin = jnp.broadcast_to(spin[None], (8, CC))
    place = jnp.stack([(lat < lats - 1).astype(jnp.int32), (lat > 0).astype(jnp.int32)])

    shape = jax.ShapeDtypeStruct
    east, west, strips, east_corner, west_corner = pl.pallas_call(
        pack_kernel,
        out_shape=[
            shape((HALO_ROWS, COLS), f32),
            shape((HALO_ROWS, COLS), f32),
            shape((GROUPS, ROWS, 128), f32),
            shape((4 * GROUPS, 128), f32),
            shape((4 * GROUPS, 128), f32),
        ],
        in_specs=[VMEM] * 3,
        out_specs=[VMEM] * 5,
        compiler_params=pltpu.CompilerParams(vmem_limit_bytes=24 << 20),
    )(saved_states, final_cotangent, sea_mask)

    def send(x, dx, dy):
        pairs = []
        for i in range(lons):
            for j in range(lats):
                if 0 <= j + dy < lats:
                    pairs.append((i * lats + j, ((i + dx) % lons) * lats + j + dy))
        return lax.ppermute(x, ("lon", "lat"), pairs)

    from_west = send(east, 1, 0)
    sw = send(east_corner, 1, 1)
    nw = send(east_corner, 1, -1)
    from_east = send(west, -1, 0)
    se = send(west_corner, -1, 1)
    ne = send(west_corner, -1, -1)
    from_south = send(strips, 0, 1)
    from_north = send(strips, 0, -1)

    return pl.pallas_call(
        step_kernel,
        out_shape=[shape((CH, ROWS, COLS), f32), shape((ROWS, COLS), f32)],
        in_specs=[SMEM, SMEM, ANY, ANY] + [VMEM] * 11,
        out_specs=[ANY, ANY],
        scratch_shapes=[
            pltpu.VMEM((PLANES, W, RR, 128), f32),
            pltpu.VMEM((CH, T, 8, CC), f32),
            pltpu.VMEM((CH, T, 8, CC), f32),
            pltpu.VMEM((L, T, 8, CC), f32),
            pltpu.VMEM((T, 8, CC), f32),
            pltpu.VMEM((W, RR, 128), jnp.int32),
            pltpu.SemaphoreType.DMA(((N + 1) * W,)),
        ],
        compiler_params=pltpu.CompilerParams(vmem_limit_bytes=40 << 20),
    )(
        place,
        gravities,
        saved_states,
        final_cotangent,
        sea_mask,
        layer_index,
        spin,
        from_west,
        from_east,
        from_south,
        from_north,
        sw,
        nw,
        se,
        ne,
    )


def solution(mesh):
    return jax.shard_map(
        per_device,
        mesh=mesh,
        in_specs=(
            P(None, None, "lon", "lat"),
            P(None, "lon", "lat"),
            P(),
            P("lon", "lat"),
            P("lon", "lat"),
        ),
        out_specs=(P(None, "lon", "lat"), P("lon", "lat")),
        check_vma=False,
    )
```

profile of v0, /device:TPU:1, one launch (start us, length us, event | category | flops | bytes accessed | tf_op | source)
XLA Modules:
  0.0 55.8 jit_solution(4557080021419996270)
XLA Ops:
  0.6 0.0 copy-start
  0.6 1.9 %copy-done = f32[4,12,32,512]{3,2,1,0:T(8,128)S(1)} copy-done((f32[4,12,32,512]{3,2,1,0:T(8,128)S(1)}, f32[4,12,32,512]{3,2,1,0:T(8,128)}, u32[]{:S(2)}) %copy-start) | copy-done | bytes 3145752
  2.5 0.0 copy-start.2
  2.5 1.1 %copy-done.2 = f32[12,32,512]{2,1,0:T(8,128)S(1)} copy-done((f32[12,32,512]{2,1,0:T(8,128)S(1)}, f32[12,32,512]{2,1,0:T(8,128)}, u32[]{:S(2)}) %copy-start.2) | copy-done | bytes 786456
  3.7 0.0 copy-start.4
  3.7 0.8 %copy-done.4 = s32[32,512]{1,0:T(8,128)S(1)} copy-done((s32[32,512]{1,0:T(8,128)S(1)}, s32[32,512]{1,0:T(8,128)}, u32[]{:S(2)}) %copy-start.4) | copy-done | bytes 65560
  4.5 0.0 copy-start.1
  4.5 0.0 copy-start.5
  4.5 1.2 %shard_map.68 = (f32[156,512]{1,0:T(8,128)}, f32[156,512]{1,0:T(8,128)}, f32[4,32,128]{2,1,0:T(8,128)S(1)}, f32[16,128]{1,0:T(8,128)}, f32[16,128]{1,0:T(8,128)}) custom-call(f32[4,12,32,512]{3,2,1,0:T(8,128)S(1)} %copy-done, f32[12,32,512]{2,1,0:T(8,128)S(1)} %copy-done.2, s32[32,512]{1,0:T(8,128)S(1)} %copy-done.4), custom_call_target="tpu_custom_call" | custom-call | tf_op jit(solution)/shard_map/pallas_call | solution.py:300
  5.7 0.0 copy-start.8
  5.7 0.6 %copy-done.8 = f32[4,32,128]{2,1,0:T(8,128)} copy-done((f32[4,32,128]{2,1,0:T(8,128)}, f32[4,32,128]{2,1,0:T(8,128)S(1)}, u32[]{:S(2)}) %copy-start.8) | copy-done | bytes 65560
  6.3 2.0 %collective-permute-start = (f32[156,512]{1,0:T(8,128)}, f32[156,512]{1,0:T(8,128)S(1)}, u32[]{:S(2)}, u32[]{:S(2)}) collective-permute-start(f32[156,512]{1,0:T(8,128)} %get-tuple-element.7), channel_id=1, source_target_pairs={{0,4},{1,5},{2,6},{3,7},{4,8},{5,9},{6,10},{7,11},{8,12},{9,13},{1... | collective-permute-start | bytes 958472 | tf_op jit(solution)/shard_map/ppermute | solution.py:320
  8.3 9.2 %collective-permute-start.1 = (f32[156,512]{1,0:T(8,128)}, f32[156,512]{1,0:T(8,128)}, u32[]{:S(2)}, u32[]{:S(2)}) collective-permute-start(f32[156,512]{1,0:T(8,128)} %get-tuple-element.8), channel_id=1, source_target_pairs={{0,252},{1,253},{2,254},{3,255},{4,0},{5,1},{6,2},{7,3},{8,4},{9,5... | collective-permute-start | bytes 958472 | tf_op jit(solution)/shard_map/ppermute | solution.py:320
  17.5 1.9 %collective-permute-start.5 = (f32[16,128]{1,0:T(8,128)}, f32[16,128]{1,0:T(8,128)S(1)}, u32[]{:S(2)}, u32[]{:S(2)}) collective-permute-start(f32[16,128]{1,0:T(8,128)} %get-tuple-element.10), channel_id=1, source_target_pairs={{1,4},{2,5},{3,6},{5,8},{6,9},{7,10},{9,12},{10,13},{11,14},{13,16... | collective-permute-start | bytes 24584 | tf_op jit(solution)/shard_map/ppermute | solution.py:320
  19.5 1.9 %collective-permute-start.4 = (f32[16,128]{1,0:T(8,128)}, f32[16,128]{1,0:T(8,128)S(1)}, u32[]{:S(2)}, u32[]{:S(2)}) collective-permute-start(f32[16,128]{1,0:T(8,128)} %get-tuple-element.10), channel_id=1, source_target_pairs={{0,5},{1,6},{2,7},{4,9},{5,10},{6,11},{8,13},{9,14},{10,15},{12,17... | collective-permute-start | bytes 24584 | tf_op jit(solution)/shard_map/ppermute | solution.py:320
  21.4 9.4 %collective-permute-start.7 = (f32[16,128]{1,0:T(8,128)}, f32[16,128]{1,0:T(8,128)}, u32[]{:S(2)}, u32[]{:S(2)}) collective-permute-start(f32[16,128]{1,0:T(8,128)} %get-tuple-element.11), channel_id=1, source_target_pairs={{1,252},{2,253},{3,254},{5,0},{6,1},{7,2},{9,4},{10,5},{11,6},{13,... | collective-permute-start | bytes 24584 | tf_op jit(solution)/shard_map/ppermute | solution.py:320
  30.8 0.6 %fusion.7 = f32[640]{0:T(1024)} fusion(s32[]{:T(128)S(6)} %mul.23), kind=kLoop, calls=%fused_computation.8 | loop fusion | flops 6400 | bytes 2564 | tf_op jit(solution)/shard_map/mul | solution.py:295
  31.4 0.0 collective-permute-done.5.nw
  31.4 4.2 %collective-permute-start.6 = (f32[16,128]{1,0:T(8,128)}, f32[16,128]{1,0:T(8,128)S(1)}, u32[]{:S(2)}, u32[]{:S(2)}) collective-permute-start(f32[16,128]{1,0:T(8,128)} %get-tuple-element.11), channel_id=1, source_target_pairs={{0,253},{1,254},{2,255},{4,1},{5,2},{6,3},{8,5},{9,6},{10,7},{12,9... | collective-permute-start | bytes 24584 | tf_op jit(solution)/shard_map/ppermute | solution.py:320
  35.7 0.0 collective-permute-done.4.sw
  35.7 2.2 %collective-permute-start.3 = (f32[4,32,128]{2,1,0:T(8,128)}, f32[4,32,128]{2,1,0:T(8,128)S(1)}, u32[]{:S(2)}, u32[]{:S(2)}) collective-permute-start(f32[4,32,128]{2,1,0:T(8,128)} %copy-done.8), channel_id=1, source_target_pairs={{1,0},{2,1},{3,2},{5,4},{6,5},{7,6},{9,8},{10,9},{11,10},{13,12},{... | collective-permute-start | bytes 196616 | tf_op jit(solution)/shard_map/ppermute | solution.py:320
  37.9 0.0 collective-permute-done.7.ne
  37.9 3.3 %collective-permute-start.2 = (f32[4,32,128]{2,1,0:T(8,128)}, f32[4,32,128]{2,1,0:T(8,128)S(1)}, u32[]{:S(2)}, u32[]{:S(2)}) collective-permute-start(f32[4,32,128]{2,1,0:T(8,128)} %copy-done.8), channel_id=1, source_target_pairs={{0,1},{1,2},{2,3},{4,5},{5,6},{6,7},{8,9},{9,10},{10,11},{12,13},{... | collective-permute-start | bytes 196616 | tf_op jit(solution)/shard_map/ppermute | solution.py:320
  41.3 0.1 add_convert_fusion.place
  41.3 0.0 collective-permute-done.6.se
  41.3 0.1 collective-permute-done.3.from_north
  41.5 1.4 %collective-permute-done.2.from_south = f32[4,32,128]{2,1,0:T(8,128)S(1)} collective-permute-done((f32[4,32,128]{2,1,0:T(8,128)}, f32[4,32,128]{2,1,0:T(8,128)S(1)}, u32[]{:S(2)}, u32[]{:S(2)}) %collective-permute-start.2) | collective-permute-done | bytes 65568 | tf_op jit(solution)/shard_map/ppermute | solution.py:320
  42.9 0.0 collective-permute-done.from_west
  42.9 0.0 collective-permute-done.1.from_east
  42.9 0.7 %broadcast_in_dim.2.spin = f32[8,640]{1,0:T(8,128)S(1)} broadcast(f32[640]{0:T(1024)} %fusion.7), dimensions={1} | broadcast | bytes 23040 | tf_op jit(solution)/shard_map/broadcast_in_dim | solution.py:296
  43.6 0.0 copy-done.1
  43.6 0.0 copy-done.5
  43.6 0.0 copy-start.3
  43.6 1.1 %copy-done.3 = f32[12,32,512]{2,1,0:T(8,128)S(1)} copy-done((f32[12,32,512]{2,1,0:T(8,128)S(1)}, f32[12,32,512]{2,1,0:T(8,128)}, u32[]{:S(2)}) %copy-start.3) | copy-done | bytes 786456
  44.7 0.0 copy-start.6
  44.7 0.8 %copy-done.6 = s32[32,512]{1,0:T(8,128)S(1)} copy-done((s32[32,512]{1,0:T(8,128)S(1)}, s32[32,512]{1,0:T(8,128)}, u32[]{:S(2)}) %copy-start.6) | copy-done | bytes 65560
  45.5 0.0 copy-start.7
  45.5 0.7 %copy-done.7 = f32[4]{0:T(128)S(1)} copy-done((f32[4]{0:T(128)S(1)}, f32[4]{0:T(128)}, u32[]{:S(2)}) %copy-start.7) | copy-done | bytes 40
  46.2 9.6 %shard_map.69 = (f32[12,32,512]{2,1,0:T(8,128)}, f32[32,512]{1,0:T(8,128)}) custom-call(s32[2]{0:T(128)S(1)} %add_convert_fusion.place, f32[4]{0:T(128)S(1)} %copy-done.7, f32[4,12,32,512]{3,2,1,0:T(8,128)S(1)} %copy-done.1, f32[12,32,512]{2,1,0:T(8,128)S(1)} %copy-done.3, s32[32,512]{1,0:T(8,128)S(1)} %copy-done.5, s32[32,512]{1,0:T(8,128)S(1)} %copy-done.6, ...), custom_call_target="tpu_custom_call" | custom-call | tf_op jit(solution)/shard_map/pallas_call | solution.py:331
Async XLA Ops:
  0.6 1.9 %copy-start = (f32[4,12,32,512]{3,2,1,0:T(8,128)S(1)}, f32[4,12,32,512]{3,2,1,0:T(8,128)}, u32[]{:S(2)}) copy-start(f32[4,12,32,512]{3,2,1,0:T(8,128)} %states.3) | copy-start | bytes 9437188
  2.5 1.1 %copy-start.2 = (f32[12,32,512]{2,1,0:T(8,128)S(1)}, f32[12,32,512]{2,1,0:T(8,128)}, u32[]{:S(2)}) copy-start(f32[12,32,512]{2,1,0:T(8,128)} %cot.3) | copy-start | bytes 2359300
  3.7 0.8 %copy-start.4 = (s32[32,512]{1,0:T(8,128)S(1)}, s32[32,512]{1,0:T(8,128)}, u32[]{:S(2)}) copy-start(s32[32,512]{1,0:T(8,128)} %sea.3) | copy-start | bytes 196612
  4.5 39.1 %copy-start.1 = (f32[4,12,32,512]{3,2,1,0:T(8,128)S(1)}, f32[4,12,32,512]{3,2,1,0:T(8,128)}, u32[]{:S(2)}) copy-start(f32[4,12,32,512]{3,2,1,0:T(8,128)} %states.3) | copy-start | bytes 9437188
  4.5 39.1 %copy-start.5 = (s32[32,512]{1,0:T(8,128)S(1)}, s32[32,512]{1,0:T(8,128)}, u32[]{:S(2)}) copy-start(s32[32,512]{1,0:T(8,128)} %sea.3) | copy-start | bytes 196612
  5.7 0.6 %copy-start.8 = (f32[4,32,128]{2,1,0:T(8,128)}, f32[4,32,128]{2,1,0:T(8,128)S(1)}, u32[]{:S(2)}) copy-start(f32[4,32,128]{2,1,0:T(8,128)S(1)} %get-tuple-element.9) | copy-start | bytes 196612
  6.3 36.6 %collective-permute-start = (f32[156,512]{1,0:T(8,128)}, f32[156,512]{1,0:T(8,128)S(1)}, u32[]{:S(2)}, u32[]{:S(2)}) collective-permute-start(f32[156,512]{1,0:T(8,128)} %get-tuple-element.7), channel_id=1, source_target_pairs={{0,4},{1,5},{2,6},{3,7},{4,8},{5,9},{6,10},{7,11},{8,12},{9,13},{1... | collective-permute-start | bytes 958472 | tf_op jit(solution)/shard_map/ppermute | solution.py:320
  8.3 34.5 %collective-permute-start.1 = (f32[156,512]{1,0:T(8,128)}, f32[156,512]{1,0:T(8,128)}, u32[]{:S(2)}, u32[]{:S(2)}) collective-permute-start(f32[156,512]{1,0:T(8,128)} %get-tuple-element.8), channel_id=1, source_target_pairs={{0,252},{1,253},{2,254},{3,255},{4,0},{5,1},{6,2},{7,3},{8,4},{9,5... | collective-permute-start | bytes 958472 | tf_op jit(solution)/shard_map/ppermute | solution.py:320
  17.5 13.9 %collective-permute-start.5 = (f32[16,128]{1,0:T(8,128)}, f32[16,128]{1,0:T(8,128)S(1)}, u32[]{:S(2)}, u32[]{:S(2)}) collective-permute-start(f32[16,128]{1,0:T(8,128)} %get-tuple-element.10), channel_id=1, source_target_pairs={{1,4},{2,5},{3,6},{5,8},{6,9},{7,10},{9,12},{10,13},{11,14},{13,16... | collective-permute-start | bytes 24584 | tf_op jit(solution)/shard_map/ppermute | solution.py:320
  19.5 16.2 %collective-permute-start.4 = (f32[16,128]{1,0:T(8,128)}, f32[16,128]{1,0:T(8,128)S(1)}, u32[]{:S(2)}, u32[]{:S(2)}) collective-permute-start(f32[16,128]{1,0:T(8,128)} %get-tuple-element.10), channel_id=1, source_target_pairs={{0,5},{1,6},{2,7},{4,9},{5,10},{6,11},{8,13},{9,14},{10,15},{12,17... | collective-permute-start | bytes 24584 | tf_op jit(solution)/shard_map/ppermute | solution.py:320
  21.4 16.5 %collective-permute-start.7 = (f32[16,128]{1,0:T(8,128)}, f32[16,128]{1,0:T(8,128)}, u32[]{:S(2)}, u32[]{:S(2)}) collective-permute-start(f32[16,128]{1,0:T(8,128)} %get-tuple-element.11), channel_id=1, source_target_pairs={{1,252},{2,253},{3,254},{5,0},{6,1},{7,2},{9,4},{10,5},{11,6},{13,... | collective-permute-start | bytes 24584 | tf_op jit(solution)/shard_map/ppermute | solution.py:320
  31.4 9.9 %collective-permute-start.6 = (f32[16,128]{1,0:T(8,128)}, f32[16,128]{1,0:T(8,128)S(1)}, u32[]{:S(2)}, u32[]{:S(2)}) collective-permute-start(f32[16,128]{1,0:T(8,128)} %get-tuple-element.11), channel_id=1, source_target_pairs={{0,253},{1,254},{2,255},{4,1},{5,2},{6,3},{8,5},{9,6},{10,7},{12,9... | collective-permute-start | bytes 24584 | tf_op jit(solution)/shard_map/ppermute | solution.py:320
  35.7 5.8 %collective-permute-start.3 = (f32[4,32,128]{2,1,0:T(8,128)}, f32[4,32,128]{2,1,0:T(8,128)S(1)}, u32[]{:S(2)}, u32[]{:S(2)}) collective-permute-start(f32[4,32,128]{2,1,0:T(8,128)} %copy-done.8), channel_id=1, source_target_pairs={{1,0},{2,1},{3,2},{5,4},{6,5},{7,6},{9,8},{10,9},{11,10},{13,12},{... | collective-permute-start | bytes 196616 | tf_op jit(solution)/shard_map/ppermute | solution.py:320
  37.9 4.9 %collective-permute-start.2 = (f32[4,32,128]{2,1,0:T(8,128)}, f32[4,32,128]{2,1,0:T(8,128)S(1)}, u32[]{:S(2)}, u32[]{:S(2)}) collective-permute-start(f32[4,32,128]{2,1,0:T(8,128)} %copy-done.8), channel_id=1, source_target_pairs={{0,1},{1,2},{2,3},{4,5},{5,6},{6,7},{8,9},{9,10},{10,11},{12,13},{... | collective-permute-start | bytes 196616 | tf_op jit(solution)/shard_map/ppermute | solution.py:320
  43.6 1.1 %copy-start.3 = (f32[12,32,512]{2,1,0:T(8,128)S(1)}, f32[12,32,512]{2,1,0:T(8,128)}, u32[]{:S(2)}) copy-start(f32[12,32,512]{2,1,0:T(8,128)} %cot.3) | copy-start | bytes 2359300
  44.7 0.8 %copy-start.6 = (s32[32,512]{1,0:T(8,128)S(1)}, s32[32,512]{1,0:T(8,128)}, u32[]{:S(2)}) copy-start(s32[32,512]{1,0:T(8,128)} %layer.1) | copy-start | bytes 196612
  45.5 0.7 %copy-start.7 = (f32[4]{0:T(128)S(1)}, f32[4]{0:T(128)}, u32[]{:S(2)}) copy-start(f32[4]{0:T(128)} %gravities.1) | copy-start | bytes 52
where the time goes:
time: 56.3 us; the launch traced here: 55.8 us
  starting transfers between devices  34.2 us (61%)
  Pallas kernels  10.8 us (19%)
  local copies, waits for them, and re-layouts  7.79 us (14%)
  waiting for transfers between devices  1.56 us (3%)
  other arithmetic  0.72 us (1%)
  between operations  0.72 us (1%)
    ppermute x8, starting transfers between devices, send(): return lax.ppermute(x, ('lon', 'lat'), pairs)  34.2 us
    pallas_call x1, Pallas kernels, per_device(): pl.pallas_call(step_kernel, out_shape=[shape((CH, ROWS, COLS), f32), shap...  9.62 us
    unnamed x18, local copies, waits for them, and re-layouts  7.12 us
    ppermute x8, waiting for transfers between devices, send(): return lax.ppermute(x, ('lon', 'lat'), pairs)  1.56 us
    pallas_call x1, Pallas kernels, per_device(): pl.pallas_call(pack_kernel, out_shape=[shape((HALO_ROWS, COLS), f32), sha...  1.18 us
  transfers between devices with their start and end apart: 8, of which 2 were waited for; matrix products, arithmetic and copies ran while one was open for 1% of the time, Pallas kernels for 0%

commit v1 on v0

v1 whole, which is shorter than its diff:
```python
import jax
import jax.numpy as jnp
from jax import lax
from jax.experimental import pallas as pl
from jax.experimental.pallas import tpu as pltpu
from jax.sharding import PartitionSpec as P

TIME_STEP = 0.3
VISCOSITY = 0.1
DIFFUSION = 0.05
BOTTOM_DRAG = 0.2

L = 4
N = 4
CH = 3 * L
ROWS = 32
COLS = 512
CC = COLS + 128
W = CC // 128
RIM = 16 + 2 * N

COT = N * CH
SEA = COT + CH
PLANES = SEA + 1
GROUPS = -(-PLANES // 16)
f32 = jnp.float32


def lanes(j):
    return slice(128 * j, 128 * j + 128)


def depth(q):
    if q >= COT:
        return N
    n, c = divmod(q, CH)
    return n + 1 if c >= L else n


OFFSET = {}
HALO = 0
for _q in sorted(range(PLANES), key=lambda q: -depth(q)):
    if depth(_q):
        OFFSET[_q] = HALO
        HALO += depth(_q)
MESSAGE = HALO + N


def start(pairs, sems):
    copies = [pltpu.make_async_copy(a, b, sems.at[i]) for i, (a, b) in enumerate(pairs)]
    for copy in copies:
        copy.start()
    return copies


def wait(copies):
    for copy in copies:
        copy.wait()


def strip_pack_kernel(states, cot, sea, strips, left, right, flags, sems):
    pairs = [(sea, flags)]
    for buf, cols in ((left, slice(0, 128)), (right, slice(COLS - 128, COLS))):
        pairs.append((states.at[:, :, :, cols], buf.at[:N]))
        pairs.append((cot.at[:, :, cols], buf.at[N]))
    wait(start(pairs, sems))
    lane = lax.broadcasted_iota(jnp.int32, (ROWS, 128), 1)
    for g in range(GROUPS):
        total = jnp.zeros((ROWS, 128), f32)
        for k in range(16):
            q = g * 16 + k
            if q >= PLANES:
                continue
            if q == SEA:
                first, last = flags[:, lanes(0)].astype(f32), flags[:, lanes(W - 2)].astype(f32)
            else:
                first, last = left[q // CH, q % CH], right[q // CH, q % CH]
            both = pltpu.roll(jnp.where(lane >= 124, last, first), (8 * k + 4) % 128, 1)
            total = jnp.where(lane // 8 == k, both, total)
        strips[g] = total


def row_pack_kernel(place, states, cot, sea, pair, middle, east, west, edge, top, bottom, flags, sems):
    pairs = [(sea, flags)]
    for buf, rows in ((top, slice(0, 8)), (bottom, slice(ROWS - 8, ROWS))):
        pairs.append((states.at[:, :, rows, :], buf.at[:N]))
        pairs.append((cot.at[:, rows, :], buf.at[N]))
    copies = start(pairs, sems)
    south = lax.broadcasted_iota(jnp.int32, (ROWS, 128), 1) % 8 < 4
    for g in range(GROUPS):
        merged = jnp.where(south == (place[0] == 1), pair[g], middle[g])
        edge[g] = merged
        east[HALO:, lanes(g)] = merged[ROWS - N :]
        west[HALO:, lanes(g)] = merged[:N]
    wait(copies)
    for q, row in OFFSET.items():
        d = depth(q)
        if q == SEA:
            east[row : row + d] = flags[ROWS - d :].astype(f32)
            west[row : row + d] = flags[:d].astype(f32)
        else:
            east[row : row + d] = bottom[q // CH, q % CH, 8 - d :]
            west[row : row + d] = top[q // CH, q % CH, :d]


def fill_halo(planes, message, first, last):
    for q, row in OFFSET.items():
        d = depth(q)
        at = first if last is None else last - d
        for j in range(W - 1):
            planes[q, j, at : at + d, :] = message[row : row + d, lanes(j)]
    at = first if last is None else last - N
    for q in range(PLANES):
        g, k = divmod(q, 16)
        planes[q, W - 1, at : at + N, :] = pltpu.roll(message[HALO:, lanes(g)], (124 - 8 * k) % 128, 1)


def fill_columns(planes, edge, blocks):
    for source, target, count in blocks:
        for q in range(PLANES):
            g, k = divmod(q, 16)
            planes[q, W - 1, target : target + count, :] = pltpu.roll(
                edge[g, source : source + count, :], (124 - 8 * k) % 128, 1
            )


def own_copies(n, source, planes, blocks, sems):
    return [
        pltpu.make_async_copy(
            source.at[:, row : row + count, lanes(j)],
            planes.at[pl.ds(n * CH, CH), j, target : target + count, :],
            sems.at[n, j, i],
        )
        for i, (row, target, count) in enumerate(blocks)
        for j in range(W - 1)
    ]


def adjoint_steps(rows, arrive, place, gravities, spin, planes, picked, cur, nxt, mixed, acc):
    T = rows // 8
    half = 0.5 * TIME_STEP

    def ring(t):
        return pl.ds(t, 8, stride=T)

    def read(q, t):
        return jnp.concatenate([planes[q, j, ring(t), :] for j in range(W)], axis=1)

    def write(q, t, value):
        for j in range(W - 1):
            planes[q, j, ring(t), :] = value[:, lanes(j)]

    for t in range(T):
        sea_t = read(SEA, t)
        for c in range(CH):
            value = read(COT + c, t)
            cur[c, t] = value if c < L else value * sea_t
        acc[t] = jnp.zeros((8, CC), f32)

    edge_lane = lax.broadcasted_iota(jnp.int32, (8, 128), 1)
    inside = jnp.where(edge_lane < 64, place[1], place[2]) > 0

    def north(x):
        return pltpu.roll(x, CC - 1, 1)

    def south(x):
        return pltpu.roll(x, 1, 1)

    def east(load, t):
        return load(t + 1) if t + 1 < T else pltpu.roll(load(0), 7, 0)

    def west(load, t):
        return load(t - 1) if t > 0 else pltpu.roll(load(T - 1), 1, 0)

    def one_step(index, src, dst):
        n = N - 1 - index
        arrive(n)

        def layer_body(k, carry):
            load_h = lambda t: read(n * CH + k, t)
            load_u = lambda t: read(n * CH + L + k, t)
            load_v = lambda t: read(n * CH + 2 * L + k, t)
            load_c = lambda t: src[k, t]
            load_p = lambda t: src[L + k, t]
            load_q = lambda t: src[2 * L + k, t]
            drag = jnp.where(k == L - 1, BOTTOM_DRAG, 0.0)
            keep = 1.0 - TIME_STEP * (4.0 * VISCOSITY + drag)
            turn = spin[...]
            for t in range(T):
                c, p, q = load_c(t), load_p(t), load_q(t)
                h, u, v = load_h(t), load_u(t), load_v(t)
                ce, cw, cn, cs = east(load_c, t), west(load_c, t), north(c), south(c)
                dcx = ce - cw
                dcy = cn - cs
                pe, pw, pn, ps = east(load_p, t), west(load_p, t), north(p), south(p)
                qe, qw, qn, qs = east(load_q, t), west(load_q, t), north(q), south(q)
                mixed[k, t] = (pe - pw) + (qn - qs)
                dst[k, t] = (1.0 - 4.0 * TIME_STEP * DIFFUSION) * c + half * (
                    u * dcx + v * dcy + (2.0 * DIFFUSION) * ((ce + cw) + (cn + cs))
                )
                ue, uw, un, us = east(load_u, t), west(load_u, t), north(u), south(u)
                ve, vw, vn, vs = east(load_v, t), west(load_v, t), north(v), south(v)
                a_e = ue + 2.0 * VISCOSITY
                a_w = 2.0 * VISCOSITY - uw
                a_n = vn + 2.0 * VISCOSITY
                a_s = 2.0 * VISCOSITY - vs
                new_p = keep * p + half * (
                    h * dcx
                    - turn * q
                    - p * (ue - uw)
                    - q * (ve - vw)
                    + (a_e * pe + a_w * pw)
                    + (a_n * pn + a_s * ps)
                )
                new_q = keep * q + half * (
                    h * dcy
                    + turn * p
                    - p * (un - us)
                    - q * (vn - vs)
                    + (a_e * qe + a_w * qw)
                    + (a_n * qn + a_s * qs)
                )
                mask = jnp.where(n == 0, 1.0, read(SEA, t))
                dst[L + k, t] = new_p * mask
                dst[2 * L + k, t] = new_q * mask
            return carry

        lax.fori_loop(0, L, layer_body, 0)
        for t in range(T):
            idx = jnp.concatenate([picked[j, ring(t), :] for j in range(W)], axis=1)
            chosen = jnp.zeros((8, CC), f32)
            for k in range(L):
                chosen = jnp.where(idx == k, src[k, t], chosen)
            acc[t] = acc[t] + TIME_STEP * chosen
            total = mixed[L - 1, t]
            tails = [total]
            for k in range(L - 2, -1, -1):
                total = total + mixed[k, t]
                tails.insert(0, total)
            head = None
            for k in range(L):
                term = (half * gravities[k]) * tails[k]
                head = term if head is None else head + term
                new = dst[k, t] + head
                dst[k, t, :, :COLS] = new[:, :COLS]
                dst[k, t, :, COLS:] = jnp.where(inside, new[:, COLS:], 0.0)

    def two_steps(i, carry):
        one_step(2 * i, cur, nxt)
        one_step(2 * i + 1, nxt, cur)
        return carry

    lax.fori_loop(0, N // 2, two_steps, 0)

    for t in range(T):
        for c in range(CH):
            write(COT + c, t, cur[c, t])
        write(SEA, t, acc[t])


def layer_copies(layer, picked, blocks):
    return [
        (layer.at[row : row + count, lanes(j)], picked.at[j, target : target + count, :])
        for row, target, count in blocks
        for j in range(W - 1)
    ]


def main_kernel(
    place,
    gravities,
    states,
    cot,
    sea,
    layer,
    spin,
    edge,
    out,
    forcing,
    planes,
    cur,
    nxt,
    mixed,
    acc,
    picked,
    flags,
    spins,
    edges,
    sems,
    more,
):
    blocks = [(0, 0, ROWS)]
    first = start([(sea, flags), (edge, edges), (spin, spins)] + layer_copies(layer, picked, blocks), more)
    copies = [own_copies(N, cot, planes, blocks, sems)]
    for n in range(N - 1, -1, -1):
        copies.append(own_copies(n, states.at[n], planes, blocks, sems))
    for group in copies:
        for copy in group:
            copy.start()
    wait(first)
    for j in range(W - 1):
        planes[SEA, j, :ROWS, :] = flags[:, lanes(j)].astype(f32)
    fill_columns(planes, edges, blocks)
    wait(copies[0])
    adjoint_steps(
        ROWS,
        lambda n: wait(own_copies(n, states.at[n], planes, blocks, sems)),
        place,
        gravities,
        spins,
        planes,
        picked,
        cur,
        nxt,
        mixed,
        acc,
    )
    pairs = []
    for j in range(W - 1):
        pairs.append((planes.at[COT : COT + CH, j, :ROWS, :], out.at[:, :, lanes(j)]))
        pairs.append((planes.at[SEA, j, :ROWS, :], forcing.at[:, lanes(j)]))
    wait(start(pairs, more))


def rim_kernel(
    place,
    gravities,
    states,
    cot,
    sea,
    layer,
    spin,
    from_west,
    from_east,
    edge,
    out_in,
    forcing_in,
    out,
    forcing,
    planes,
    cur,
    nxt,
    mixed,
    acc,
    picked,
    flags,
    spins,
    edges,
    wests,
    easts,
    tiles,
    sems,
    more,
):
    blocks = [(ROWS - 8, 0, 8), (0, RIM - 8, 8)]
    late = start([(from_west, wests), (from_east, easts)], more.at[:2])
    first = start([(sea, flags), (edge, edges), (spin, spins)] + layer_copies(layer, picked, blocks), more.at[2:])
    copies = [own_copies(N, cot, planes, blocks, sems)]
    for n in range(N - 1, -1, -1):
        copies.append(own_copies(n, states.at[n], planes, blocks, sems))
    for group in copies:
        for copy in group:
            copy.start()
    back = []
    for i, (row, _, _) in enumerate(blocks):
        back.append((out_in.at[:, row : row + 8, :], tiles.at[i, :CH]))
        back.append((forcing_in.at[row : row + 8, :], tiles.at[i, CH]))
    back = start(back, more.at[13:])
    wait(first)
    for row, target, _ in blocks:
        for j in range(W - 1):
            planes[SEA, j, target : target + 8, :] = flags[row : row + 8, lanes(j)].astype(f32)
    fill_columns(planes, edges, blocks)
    wait(late)
    fill_halo(planes, easts, 8, None)
    fill_halo(planes, wests, None, RIM - 8)
    wait(copies[0])
    adjoint_steps(
        RIM,
        lambda n: wait(own_copies(n, states.at[n], planes, blocks, sems)),
        place,
        gravities,
        spins,
        planes,
        picked,
        cur,
        nxt,
        mixed,
        acc,
    )
    wait(back)
    sublane = lax.broadcasted_iota(jnp.int32, (8, 128), 0)
    pairs = []
    for i, (row, target, _) in enumerate(blocks):
        late_row = sublane >= N if row else sublane < N
        for c in range(CH + 1):
            for j in range(W - 1):
                tiles[i, c, :, lanes(j)] = jnp.where(
                    late_row, planes[COT + c, j, target : target + 8, :], tiles[i, c, :, lanes(j)]
                )
        pairs.append((tiles.at[i, :CH], out.at[:, row : row + 8, :]))
        pairs.append((tiles.at[i, CH], forcing.at[row : row + 8, :]))
    wait(start(pairs, more))


VMEM = pl.BlockSpec(memory_space=pltpu.VMEM)
SMEM = pl.BlockSpec(memory_space=pltpu.SMEM)
ANY = pl.BlockSpec(memory_space=pl.ANY)
HBM = pl.BlockSpec(memory_space=pltpu.HBM)
DMA = pltpu.SemaphoreType.DMA
shape = jax.ShapeDtypeStruct


def ring_scratch(rows):
    T = rows // 8
    return [
        pltpu.VMEM((PLANES, W, rows, 128), f32),
        pltpu.VMEM((CH, T, 8, CC), f32),
        pltpu.VMEM((CH, T, 8, CC), f32),
        pltpu.VMEM((L, T, 8, CC), f32),
        pltpu.VMEM((T, 8, CC), f32),
        pltpu.VMEM((W, rows, 128), jnp.int32),
        pltpu.VMEM((ROWS, COLS), jnp.int32),
        pltpu.VMEM((8, CC), f32),
        pltpu.VMEM((GROUPS, ROWS, 128), f32),
    ]


def per_device(saved_states, final_cotangent, gravities, sea_mask, layer_index):
    lons, lats = lax.axis_size("lon"), lax.axis_size("lat")
    lat = lax.axis_index("lat")
    lane = jnp.arange(CC, dtype=jnp.int32)
    lane = jnp.where(lane < COLS + 64, lane, lane - CC)
    lat_rows = (lat * COLS + lane).astype(f32)
    spin = 2.0 * jnp.sin(jnp.pi * ((lat_rows + 0.5) / (lats * COLS) - 0.5))
    spin = jnp.broadcast_to(spin[None], (8, CC))
    place = jnp.stack([lat % 2, (lat < lats - 1).astype(jnp.int32), (lat > 0).astype(jnp.int32)])

    strips = pl.pallas_call(
        strip_pack_kernel,
        out_shape=shape((GROUPS, ROWS, 128), f32),
        in_specs=[HBM] * 3,
        out_specs=VMEM,
        scratch_shapes=[
            pltpu.VMEM((N + 1, CH, ROWS, 128), f32),
            pltpu.VMEM((N + 1, CH, ROWS, 128), f32),
            pltpu.VMEM((ROWS, COLS), jnp.int32),
            DMA((5,)),
        ],
        compiler_params=pltpu.CompilerParams(vmem_limit_bytes=60 << 20),
    )(saved_states, final_cotangent, sea_mask)

    def at(i, j):
        return (i % lons) * lats + j

    def swap(x, first):
        pairs = [(at(i, j), at(i, j + 1)) for i in range(lons) for j in range(first, lats - 1, 2)]
        return lax.ppermute(x, ("lon", "lat"), pairs + [(b, a) for a, b in pairs])

    def shift(x, by):
        return lax.ppermute(x, "lon", [(i, (i + by) % lons) for i in range(lons)])

    pair, middle = swap(strips, 0), swap(strips, 1)
    east, west, edge = pl.pallas_call(
        row_pack_kernel,
        out_shape=[shape((MESSAGE, COLS), f32), shape((MESSAGE, COLS), f32), shape((GROUPS, ROWS, 128), f32)],
        in_specs=[SMEM, HBM, HBM, HBM, VMEM, VMEM],
        out_specs=[VMEM] * 3,
        scratch_shapes=[
            pltpu.VMEM((N + 1, CH, 8, COLS), f32),
            pltpu.VMEM((N + 1, CH, 8, COLS), f32),
            pltpu.VMEM((ROWS, COLS), jnp.int32),
            DMA((5,)),
        ],
        compiler_params=pltpu.CompilerParams(vmem_limit_bytes=53 << 20),
    )(place, saved_states, final_cotangent, sea_mask, pair, middle)
    from_west, from_east = shift(east, 1), shift(west, -1)

    outs = [shape((CH, ROWS, COLS), f32), shape((ROWS, COLS), f32)]
    out, forcing = pl.pallas_call(
        main_kernel,
        out_shape=outs,
        in_specs=[SMEM, SMEM] + [HBM] * 4 + [ANY] * 2,
        out_specs=[HBM, HBM],
        scratch_shapes=ring_scratch(ROWS) + [DMA((N + 1, W - 1, 1)), DMA((16,))],
        compiler_params=pltpu.CompilerParams(vmem_limit_bytes=53 << 20),
        cost_estimate=pl.CostEstimate(flops=160_000_000, bytes_accessed=24_000_000, transcendentals=0),
    )(place, gravities, saved_states, final_cotangent, sea_mask, layer_index, spin, edge)

    return pl.pallas_call(
        rim_kernel,
        out_shape=outs,
        in_specs=[SMEM, SMEM] + [HBM] * 4 + [ANY] * 4 + [HBM] * 2,
        out_specs=[HBM, HBM],
        scratch_shapes=ring_scratch(RIM)
        + [
            pltpu.VMEM((MESSAGE, COLS), f32),
            pltpu.VMEM((MESSAGE, COLS), f32),
            pltpu.VMEM((2, CH + 1, 8, COLS), f32),
            DMA((N + 1, W - 1, 2)),
            DMA((20,)),
        ],
        input_output_aliases={10: 0, 11: 1},
        compiler_params=pltpu.CompilerParams(vmem_limit_bytes=53 << 20),
    )(
        place,
        gravities,
        saved_states,
        final_cotangent,
        sea_mask,
        layer_index,
        spin,
        from_west,
        from_east,
        edge,
        out,
        forcing,
    )


def solution(mesh):
    return jax.shard_map(
        per_device,
        mesh=mesh,
        in_specs=(
            P(None, None, "lon", "lat"),
            P(None, "lon", "lat"),
            P(),
            P("lon", "lat"),
            P("lon", "lat"),
        ),
        out_specs=(P(None, "lon", "lat"), P("lon", "lat")),
        check_vma=False,
    )
```

time: 56.3 us -> 39.9 us (0.71)
  starting transfers between devices: 34.2 us -> 15.1 us
  Pallas kernels: 10.8 us -> 21.7 us
  local copies, waits for them, and re-layouts: 7.79 us -> 0.02 us
  other arithmetic: 0.72 us -> 0.13 us
    ppermute x8 -> x4, starting transfers between devices: 34.2 us -> 15.1 us  [the longest x2 10.4 us: shift(): return lax.ppermute(x, 'lon', [(i, (i + by) % lons) for i in range(lons)])]
    pallas_call x2 -> x4, Pallas kernels: 10.8 us -> 21.7 us  [the longest x1 8.91 us: per_device(): pl.pallas_call(main_kernel, out_shape=outs, in_specs=[SMEM, SMEM] + [HBM]...]
    unnamed x18 -> x6, local copies, waits for them, and re-layouts: 7.12 us -> 0.01 us
    broadcast_in_dim x1, local copies, waits for them, and re-layouts: 0.68 us -> 0.01 us  [per_device(): spin = jnp.broadcast_to(spin[None], (8, CC))]
    mul x1, other arithmetic: 0.64 us -> 0.05 us  [per_device(): spin = 2.0 * jnp.sin(jnp.pi * ((lat_rows + 0.5) / (lats * COLS) - 0.5))]
    ppermute x8 -> x4, waiting for transfers between devices: 1.56 us -> 1.96 us  [the longest x2 1.96 us: swap(): return lax.ppermute(x, ('lon', 'lat'), pairs + [(b, a) for a, b in pairs])]
  transfers between devices with their start and end apart: 8 -> 4, of which waited for: 2 -> 1; matrix products, arithmetic and copies ran while one was open for 1% -> 0% of each run, Pallas kernels for 0% -> 22%
where the time goes in v1:
time: 39.9 us; the launch traced here: 39.7 us
  Pallas kernels  21.7 us (54%)
  starting transfers between devices  15.1 us (38%)
  waiting for transfers between devices  1.96 us (5%)
  between operations  0.75 us (2%)
    ppermute x2, starting transfers between devices, shift(): return lax.ppermute(x, 'lon', [(i, (i + by) % lons) for i in range(lons)])  10.4 us
    pallas_call x1, Pallas kernels, per_device(): pl.pallas_call(main_kernel, out_shape=outs, in_specs=[SMEM, SMEM] + [HBM]...  8.91 us
    pallas_call x1, Pallas kernels, per_device(): pl.pallas_call(rim_kernel, out_shape=outs, in_specs=[SMEM, SMEM] + [HBM]...  7.95 us
    ppermute x2, starting transfers between devices, swap(): return lax.ppermute(x, ('lon', 'lat'), pairs + [(b, a) for a, b in pairs])  4.69 us
    pallas_call x1, Pallas kernels, per_device(): pl.pallas_call(strip_pack_kernel, out_shape=shape((GROUPS, ROWS, 128), f3...  2.57 us
    pallas_call x1, Pallas kernels, per_device(): pl.pallas_call(row_pack_kernel, out_shape=[shape((MESSAGE, COLS), f32), s...  2.3 us
    ppermute x2, waiting for transfers between devices, swap(): return lax.ppermute(x, ('lon', 'lat'), pairs + [(b, a) for a, b in pairs])  1.96 us
  transfers between devices with their start and end apart: 4, of which 1 were waited for; matrix products, arithmetic and copies ran while one was open for 0% of the time, Pallas kernels for 22%

profile of v1, /device:TPU:1, one launch (start us, length us, event | category | flops | bytes accessed | tf_op | source)
XLA Modules:
  0.0 39.7 jit_solution(8174913914630447834)
XLA Ops:
  0.6 0.0 copy-start
  0.6 0.0 copy-start.1
  0.7 0.0 copy-start.2
  0.7 2.6 %shard_map.68 = f32[4,32,128]{2,1,0:T(8,128)} custom-call(f32[4,12,32,512]{3,2,1,0:T(8,128)} %states.7, f32[12,32,512]{2,1,0:T(8,128)} %cot.7, s32[32,512]{1,0:T(8,128)} %sea.7), custom_call_target="tpu_custom_call" | custom-call | tf_op jit(solution)/shard_map/pallas_call | solution.py:439
  3.2 4.6 %collective-permute-start.1 = (f32[4,32,128]{2,1,0:T(8,128)}, f32[4,32,128]{2,1,0:T(8,128)S(1)}, u32[]{:S(2)}, u32[]{:S(2)}) collective-permute-start(f32[4,32,128]{2,1,0:T(8,128)} %shard_map.68), channel_id=1, source_target_pairs={{1,2},{5,6},{9,10},{13,14},{17,18},{21,22},{25,26},{29,30},{33,34}... | collective-permute-start | bytes 196616 | tf_op jit(solution)/shard_map/ppermute | solution.py:458
  7.8 0.1 collective-permute-start
  8.0 0.1 pad_add_fusion.place
  8.0 2.0 %collective-permute-done.1.middle = f32[4,32,128]{2,1,0:T(8,128)S(1)} collective-permute-done((f32[4,32,128]{2,1,0:T(8,128)}, f32[4,32,128]{2,1,0:T(8,128)S(1)}, u32[]{:S(2)}, u32[]{:S(2)}) %collective-permute-start.1) | collective-permute-done | bytes 65568 | tf_op jit(solution)/shard_map/ppermute | solution.py:458
  10.0 0.0 collective-permute-done.pair
  10.0 0.0 copy-done
  10.0 2.3 %shard_map.69 = (f32[160,512]{1,0:T(8,128)S(1)}, f32[160,512]{1,0:T(8,128)S(1)}, f32[4,32,128]{2,1,0:T(8,128)S(1)}) custom-call(s32[3]{0:T(128)S(1)} %pad_add_fusion.place, f32[4,12,32,512]{3,2,1,0:T(8,128)} %states.7, f32[12,32,512]{2,1,0:T(8,128)} %cot.7, s32[32,512]{1,0:T(8,128)S(1)} %copy-done, f32[4,32,128]{2,1,0:T(8,128)S(1)} %collective-permute-done.pair, ...), custom_call_target="tpu_custom_call" | custom-call | tf_op jit(solution)/shard_map/pallas_call | solution.py:464
  12.3 1.3 %collective-permute-start.2 = (f32[160,512]{1,0:T(8,128)S(1)}, f32[160,512]{1,0:T(8,128)S(1)}, u32[]{:S(2)}, u32[]{:S(2)}) collective-permute-start(f32[160,512]{1,0:T(8,128)S(1)} %get-tuple-element.7), channel_id=1, source_target_pairs={{0,4},{4,8},{8,12},{12,16},{16,20},{20,24},{24,28},{28,32},{32,36}... | collective-permute-start | bytes 983048 | tf_op jit(solution)/shard_map/ppermute | solution.py:461
  13.6 9.2 %collective-permute-start.3 = (f32[160,512]{1,0:T(8,128)S(1)}, f32[160,512]{1,0:T(8,128)S(1)}, u32[]{:S(2)}, u32[]{:S(2)}) collective-permute-start(f32[160,512]{1,0:T(8,128)S(1)} %get-tuple-element.8), channel_id=1, source_target_pairs={{0,252},{4,0},{8,4},{12,8},{16,12},{20,16},{24,20},{28,24},{32,28}... | collective-permute-start | bytes 983048 | tf_op jit(solution)/shard_map/ppermute | solution.py:461
  22.8 0.0 copy-done.1
  22.8 0.0 copy-done.2
  22.8 8.9 %shard_map.70 = (f32[12,32,512]{2,1,0:T(8,128)}, f32[32,512]{1,0:T(8,128)}) custom-call(s32[3]{0:T(128)S(1)} %pad_add_fusion.place, f32[4]{0:T(128)S(1)} %copy-done.2, f32[4,12,32,512]{3,2,1,0:T(8,128)} %states.7, f32[12,32,512]{2,1,0:T(8,128)} %cot.7, s32[32,512]{1,0:T(8,128)S(1)} %copy-done, s32[32,512]{1,0:T(8,128)S(1)} %copy-done.1, ...), custom_call_target="tpu_custom_call" | custom-call | flops 160000000 | bytes 24000000 | tf_op jit(solution)/shard_map/pallas_call | solution.py:480
  31.7 0.0 collective-permute-done.2.from_west
  31.8 0.0 collective-permute-done.3.from_east
  31.8 8.0 %shard_map.71 = (f32[12,32,512]{2,1,0:T(8,128)}, f32[32,512]{1,0:T(8,128)}) custom-call(s32[3]{0:T(128)S(1)} %pad_add_fusion.place, f32[4]{0:T(128)S(1)} %copy-done.2, f32[4,12,32,512]{3,2,1,0:T(8,128)} %states.7, f32[12,32,512]{2,1,0:T(8,128)} %cot.7, s32[32,512]{1,0:T(8,128)S(1)} %copy-done, ...), custom_call_target="tpu_custom_call", output_to_operand_aliasing={{0}: (10, {}), {1}: (11, {})} | custom-call | tf_op jit(solution)/shard_map/pallas_call | solution.py:490
  (2 shorter events, 0.1 us)
Async XLA Ops:
  0.6 9.4 %copy-start = (s32[32,512]{1,0:T(8,128)S(1)}, s32[32,512]{1,0:T(8,128)}, u32[]{:S(2)}) copy-start(s32[32,512]{1,0:T(8,128)} %sea.7) | copy-start | bytes 196612
  0.6 22.2 %copy-start.1 = (s32[32,512]{1,0:T(8,128)S(1)}, s32[32,512]{1,0:T(8,128)}, u32[]{:S(2)}) copy-start(s32[32,512]{1,0:T(8,128)} %layer.3) | copy-start | bytes 196612
  0.7 22.2 %copy-start.2 = (f32[4]{0:T(128)S(1)}, f32[4]{0:T(128)}, u32[]{:S(2)}) copy-start(f32[4]{0:T(128)} %gravities.3) | copy-start | bytes 52
  3.2 6.7 %collective-permute-start.1 = (f32[4,32,128]{2,1,0:T(8,128)}, f32[4,32,128]{2,1,0:T(8,128)S(1)}, u32[]{:S(2)}, u32[]{:S(2)}) collective-permute-start(f32[4,32,128]{2,1,0:T(8,128)} %shard_map.68), channel_id=1, source_target_pairs={{1,2},{5,6},{9,10},{13,14},{17,18},{21,22},{25,26},{29,30},{33,34}... | collective-permute-start | bytes 196616 | tf_op jit(solution)/shard_map/ppermute | solution.py:458
  7.8 2.1 %collective-permute-start = (f32[4,32,128]{2,1,0:T(8,128)}, f32[4,32,128]{2,1,0:T(8,128)S(1)}, u32[]{:S(2)}, u32[]{:S(2)}) collective-permute-start(f32[4,32,128]{2,1,0:T(8,128)} %shard_map.68), channel_id=1, source_target_pairs={{0,1},{2,3},{4,5},{6,7},{8,9},{10,11},{12,13},{14,15},{16,17},{18,... | collective-permute-start | bytes 196616 | tf_op jit(solution)/shard_map/ppermute | solution.py:458
  12.3 19.4 %collective-permute-start.2 = (f32[160,512]{1,0:T(8,128)S(1)}, f32[160,512]{1,0:T(8,128)S(1)}, u32[]{:S(2)}, u32[]{:S(2)}) collective-permute-start(f32[160,512]{1,0:T(8,128)S(1)} %get-tuple-element.7), channel_id=1, source_target_pairs={{0,4},{4,8},{8,12},{12,16},{16,20},{20,24},{24,28},{28,32},{32,36}... | collective-permute-start | bytes 983048 | tf_op jit(solution)/shard_map/ppermute | solution.py:461
  13.6 18.2 %collective-permute-start.3 = (f32[160,512]{1,0:T(8,128)S(1)}, f32[160,512]{1,0:T(8,128)S(1)}, u32[]{:S(2)}, u32[]{:S(2)}) collective-permute-start(f32[160,512]{1,0:T(8,128)S(1)} %get-tuple-element.8), channel_id=1, source_target_pairs={{0,252},{4,0},{8,4},{12,8},{16,12},{20,16},{24,20},{28,24},{32,28}... | collective-permute-start | bytes 983048 | tf_op jit(solution)/shard_map/ppermute | solution.py:461

commit v2 on v1

--- a/solution.py
+++ b/solution.py
@@ -17,7 +17,6 @@
 COLS = 512
 CC = COLS + 128
 W = CC // 128
-RIM = 16 + 2 * N
 
 COT = N * CH
 SEA = COT + CH
@@ -337,13 +336,15 @@
     forcing_in,
     out,
     forcing,
-    planes,
+    own,
+    fields,
     cur,
     nxt,
-    mixed,
+    mask,
     acc,
     picked,
     flags,
+    layers,
     spins,
     edges,
     wests,
@@ -352,55 +353,171 @@
     sems,
     more,
 ):
-    blocks = [(ROWS - 8, 0, 8), (0, RIM - 8, 8)]
-    late = start([(from_west, wests), (from_east, easts)], more.at[:2])
-    first = start([(sea, flags), (edge, edges), (spin, spins)] + layer_copies(layer, picked, blocks), more.at[2:])
-    copies = [own_copies(N, cot, planes, blocks, sems)]
-    for n in range(N - 1, -1, -1):
-        copies.append(own_copies(n, states.at[n], planes, blocks, sems))
-    for group in copies:
-        for copy in group:
-            copy.start()
+    first = start([(from_west, wests), (from_east, easts), (edge, edges), (sea, flags), (layer, layers), (spin, spins)], more)
+    copies = {}
+    for n in range(N, -1, -1):
+        source = cot if n == N else states.at[n]
+        copies[n] = start(
+            [(source.at[:, :8, :], own.at[n, 0]), (source.at[:, ROWS - 8 :, :], own.at[n, 1])], sems.at[n]
+        )
     back = []
-    for i, (row, _, _) in enumerate(blocks):
-        back.append((out_in.at[:, row : row + 8, :], tiles.at[i, :CH]))
-        back.append((forcing_in.at[row : row + 8, :], tiles.at[i, CH]))
-    back = start(back, more.at[13:])
+    for e, row in enumerate((0, ROWS - 8)):
+        back.append((out_in.at[:, row : row + 8, :], tiles.at[e, :CH]))
+        back.append((forcing_in.at[row : row + 8, :], tiles.at[e, CH]))
+    back = start(back, more.at[6:])
     wait(first)
-    for row, target, _ in blocks:
+
+    def put(target, at, q, e, s):
+        g, k = divmod(q, 16)
+        d = depth(q)
+        tile = slice(0, 8) if e == 0 else slice(ROWS - 8, ROWS)
+        message = (wests, easts)[e]
+        here = 4 if e == 0 else 0
+        halo = 4 - d if e == 0 else 8
         for j in range(W - 1):
-            planes[SEA, j, target : target + 8, :] = flags[row : row + 8, lanes(j)].astype(f32)
-    fill_columns(planes, edges, blocks)
-    wait(late)
-    fill_halo(planes, easts, 8, None)
-    fill_halo(planes, wests, None, RIM - 8)
-    wait(copies[0])
-    adjoint_steps(
-        RIM,
-        lambda n: wait(own_copies(n, states.at[n], planes, blocks, sems)),
-        place,
-        gravities,
-        spins,
-        planes,
-        picked,
-        cur,
-        nxt,
-        mixed,
-        acc,
-    )
+            if q == SEA:
+                value = flags[tile, lanes(j)].astype(f32)
+            else:
+                value = own[q // CH, e, q % CH, :, lanes(j)]
+            target[at, j, pl.ds(8 * here + s, 8, stride=8), :] = value
+            if d:
+                value = message[OFFSET[q] : OFFSET[q] + d, lanes(j)]
+                target[at, j, pl.ds(8 * halo + s, d, stride=8), :] = value
+        shift = (124 - 8 * k) % 128
+        target[at, W - 1, pl.ds(8 * here + s, 8, stride=8), :] = pltpu.roll(edges[g, tile, :], shift, 1)
+        corner = pltpu.roll(message[HALO:, lanes(g)], shift, 1)
+        target[at, W - 1, pl.ds(8 * (0 if e == 0 else 8) + s, 4, stride=8), :] = corner
+
+    for e in range(2):
+        for k in range(L):
+            put(mask, 0, SEA, e, 2 * k + e)
+            for j in range(W - 1):
+                tile = slice(0, 4) if e == 0 else slice(ROWS - 4, ROWS)
+                picked[j, pl.ds(2 * k + e, 4, stride=8), :] = layers[tile, lanes(j)]
+    wait(copies[N])
+    for e in range(2):
+        for c in range(CH):
+            put(cur, c // L, COT + c, e, 2 * (c % L) + e)
+
+    half = 0.5 * TIME_STEP
+    level = lax.broadcasted_iota(jnp.int32, (8, CC), 0) // 2
+    sums = []
+    for k in range(L):
+        sums.append(gravities[k] if k == 0 else sums[-1] + gravities[k])
+    couple = []
+    for m in range(L):
+        weight = jnp.zeros((8, CC), f32)
+        for k in range(L):
+            weight = jnp.where(level == k, half * sums[min(k, (k - m) % L)], weight)
+        couple.append(weight)
+    keep = jnp.where(level == L - 1, 1.0 - TIME_STEP * (4.0 * VISCOSITY + BOTTOM_DRAG), 1.0 - TIME_STEP * 4.0 * VISCOSITY)
+    edge_lane = lax.broadcasted_iota(jnp.int32, (8, 128), 1)
+    inside = jnp.where(edge_lane < 64, place[1], place[2]) > 0
+
+    def row(ref, at, r):
+        return jnp.concatenate([ref[at, j, pl.ds(pl.multiple_of(8 * r, 8), 8), :] for j in range(W)], axis=1)
+
+    def set_row(ref, at, r, value):
+        for j in range(W):
+            ref[at, j, pl.ds(pl.multiple_of(8 * r, 8), 8), :] = value[:, lanes(j)]
+
+    def north(x):
+        return pltpu.roll(x, CC - 1, 1)
+
+    def south(x):
+        return pltpu.roll(x, 1, 1)
+
+    for r in range(12):
+        sea_r = row(mask, 0, r)
+        for at in (1, 2):
+            set_row(cur, at, r, row(cur, at, r) * sea_r)
+    for r in range(4):
+        acc[r] = jnp.zeros((8, COLS), f32)
+
+    for i in range(N):
+        n = N - 1 - i
+        src, dst = (cur, nxt) if i % 2 == 0 else (nxt, cur)
+        wait(copies[n])
+        for e in range(2):
+            for c in range(CH):
+                put(fields, c // L, n * CH + c, e, 2 * (c % L) + e)
+
+        for r in range(4):
+            idx = jnp.concatenate([picked[j, 8 * r : 8 * r + 8, :] for j in range(W - 1)], axis=1)
+            acc[r] = acc[r] + jnp.where(idx == level[:, :COLS], TIME_STEP * row(src, 0, 4 + r)[:, :COLS], 0.0)
+
+        def one_row(r):
+            c, p, q = row(src, 0, r), row(src, 1, r), row(src, 2, r)
+            h, u, v = row(fields, 0, r), row(fields, 1, r), row(fields, 2, r)
+            ce, cw, cn, cs = row(src, 0, r + 1), row(src, 0, r - 1), north(c), south(c)
+            pe, pw, pn, ps = row(src, 1, r + 1), row(src, 1, r - 1), north(p), south(p)
+            qe, qw, qn, qs = row(src, 2, r + 1), row(src, 2, r - 1), north(q), south(q)
+            ue, uw, un, us = row(fields, 1, r + 1), row(fields, 1, r - 1), north(u), south(u)
+            ve, vw, vn, vs = row(fields, 2, r + 1), row(fields, 2, r - 1), north(v), south(v)
+            dcx = ce - cw
+            dcy = cn - cs
+            mixed = (pe - pw) + (qn - qs)
+            new = (1.0 - 4.0 * TIME_STEP * DIFFUSION) * c + half * (
+                u * dcx + v * dcy + (2.0 * DIFFUSION) * ((ce + cw) + (cn + cs))
+            )
+            for m in range(L):
+                new = new + couple[m] * (mixed if m == 0 else pltpu.roll(mixed, 2 * m, 0))
+            new = jnp.concatenate([new[:, :COLS], jnp.where(inside, new[:, COLS:], 0.0)], axis=1)
+            set_row(dst, 0, r, new)
+            a_e = ue + 2.0 * VISCOSITY
+            a_w = 2.0 * VISCOSITY - uw
+            a_n = vn + 2.0 * VISCOSITY
+            a_s = 2.0 * VISCOSITY - vs
+            turn = spins[...]
+            new_p = keep * p + half * (
+                h * dcx
+                - turn * q
+                - p * (ue - uw)
+                - q * (ve - vw)
+                + (a_e * pe + a_w * pw)
+                + (a_n * pn + a_s * ps)
+            )
+            new_q = keep * q + half * (
+                h * dcy
+                + turn * p
+                - p * (un - us)
+                - q * (vn - vs)
+                + (a_e * qe + a_w * qw)
+                + (a_n * qn + a_s * qs)
+            )
+            if n:
+                sea_r = row(mask, 0, r)
+                new_p, new_q = new_p * sea_r, new_q * sea_r
+            set_row(dst, 1, r, new_p)
+            set_row(dst, 2, r, new_q)
+
+        def rows_body(b, carry):
+            one_row(1 + i + 2 * b)
+            one_row(2 + i + 2 * b)
+            return carry
+
+        lax.fori_loop(0, 5 - i, rows_body, 0)
+
     wait(back)
-    sublane = lax.broadcasted_iota(jnp.int32, (8, 128), 0)
     pairs = []
-    for i, (row, target, _) in enumerate(blocks):
-        late_row = sublane >= N if row else sublane < N
-        for c in range(CH + 1):
+    for e, start_row in enumerate((0, ROWS - 8)):
+        part = slice(0, 4) if e == 0 else slice(4, 8)
+        for c in range(CH):
             for j in range(W - 1):
-                tiles[i, c, :, lanes(j)] = jnp.where(
-                    late_row, planes[COT + c, j, target : target + 8, :], tiles[i, c, :, lanes(j)]
-                )
-        pairs.append((tiles.at[i, :CH], out.at[:, row : row + 8, :]))
-        pairs.append((tiles.at[i, CH], forcing.at[row : row + 8, :]))
-    wait(start(pairs, more))
+                tiles[e, c, part, lanes(j)] = cur[c // L, j, pl.ds(32 + 2 * (c % L) + e, 4, stride=8), :]
+        pairs.append((tiles.at[e, :CH], out.at[:, start_row : start_row + 8, :]))
+    copies = start(pairs, more)
+    pairs = []
+    for e, start_row in enumerate((0, ROWS - 8)):
+        for r in range(4):
+            total = acc[r]
+            total = total + pltpu.roll(total, 4, 0)
+            total = total + pltpu.roll(total, 2, 0)
+            at = r if e == 0 else 4 + r
+            tiles[e, CH, at : at + 1, :] = total[e : e + 1, :]
+        pairs.append((tiles.at[e, CH], forcing.at[start_row : start_row + 8, :]))
+    copies = copies + start(pairs, more.at[2:])
+    wait(copies)
 
 
 VMEM = pl.BlockSpec(memory_space=pltpu.VMEM)
@@ -492,13 +609,23 @@
         out_shape=outs,
         in_specs=[SMEM, SMEM] + [HBM] * 4 + [ANY] * 4 + [HBM] * 2,
         out_specs=[HBM, HBM],
-        scratch_shapes=ring_scratch(RIM)
-        + [
+        scratch_shapes=[
+            pltpu.VMEM((N + 1, 2, CH, 8, COLS), f32),
+            pltpu.VMEM((3, W, 96, 128), f32),
+            pltpu.VMEM((3, W, 96, 128), f32),
+            pltpu.VMEM((3, W, 96, 128), f32),
+            pltpu.VMEM((1, W, 96, 128), f32),
+            pltpu.VMEM((4, 8, COLS), f32),
+            pltpu.VMEM((W - 1, 32, 128), jnp.int32),
+            pltpu.VMEM((ROWS, COLS), jnp.int32),
+            pltpu.VMEM((ROWS, COLS), jnp.int32),
+            pltpu.VMEM((8, CC), f32),
+            pltpu.VMEM((GROUPS, ROWS, 128), f32),
             pltpu.VMEM((MESSAGE, COLS), f32),
             pltpu.VMEM((MESSAGE, COLS), f32),
             pltpu.VMEM((2, CH + 1, 8, COLS), f32),
-            DMA((N + 1, W - 1, 2)),
-            DMA((20,)),
+            DMA((N + 1, 2)),
+            DMA((10,)),
         ],
         input_output_aliases={10: 0, 11: 1},
         compiler_params=pltpu.CompilerParams(vmem_limit_bytes=53 << 20),

time: 39.9 us -> 39 us (0.977)
  Pallas kernels: 21.7 us -> 20.9 us
    pallas_call x1, Pallas kernels: 7.95 us -> 7.09 us  [per_device(): pl.pallas_call(rim_kernel, out_shape=outs, in_specs=[SMEM, SMEM] + [HBM]...]
  transfers between devices with their start and end apart: 4 -> 4, of which waited for: 1 -> 1; matrix products, arithmetic and copies ran while one was open for 0% -> 0% of each run, Pallas kernels for 22% -> 23%
where the time goes in v2:
time: 39 us; the launch traced here: 38.9 us
  Pallas kernels  20.9 us (54%)
  starting transfers between devices  15.1 us (39%)
  waiting for transfers between devices  1.96 us (5%)
  between operations  0.75 us (2%)
    ppermute x2, starting transfers between devices, shift(): return lax.ppermute(x, 'lon', [(i, (i + by) % lons) for i in range(lons)])  10.4 us
    pallas_call x1, Pallas kernels, per_device(): pl.pallas_call(main_kernel, out_shape=outs, in_specs=[SMEM, SMEM] + [HBM]...  8.91 us
    pallas_call x1, Pallas kernels, per_device(): pl.pallas_call(rim_kernel, out_shape=outs, in_specs=[SMEM, SMEM] + [HBM]...  7.09 us
    ppermute x2, starting transfers between devices, swap(): return lax.ppermute(x, ('lon', 'lat'), pairs + [(b, a) for a, b in pairs])  4.69 us
    pallas_call x1, Pallas kernels, per_device(): pl.pallas_call(strip_pack_kernel, out_shape=shape((GROUPS, ROWS, 128), f3...  2.57 us
    pallas_call x1, Pallas kernels, per_device(): pl.pallas_call(row_pack_kernel, out_shape=[shape((MESSAGE, COLS), f32), s...  2.3 us
    ppermute x2, waiting for transfers between devices, swap(): return lax.ppermute(x, ('lon', 'lat'), pairs + [(b, a) for a, b in pairs])  1.96 us
  transfers between devices with their start and end apart: 4, of which 1 were waited for; matrix products, arithmetic and copies ran while one was open for 0% of the time, Pallas kernels for 23%

profile of v2, /device:TPU:1, one launch (start us, length us, event | category | flops | bytes accessed | tf_op | source)
XLA Modules:
  0.0 38.9 jit_solution(9662999283388893807)
XLA Ops:
  0.6 0.0 copy-start
  0.6 0.0 copy-start.1
  0.7 0.0 copy-start.2
  0.7 2.6 %shard_map.68 = f32[4,32,128]{2,1,0:T(8,128)} custom-call(f32[4,12,32,512]{3,2,1,0:T(8,128)} %states.7, f32[12,32,512]{2,1,0:T(8,128)} %cot.7, s32[32,512]{1,0:T(8,128)} %sea.7), custom_call_target="tpu_custom_call" | custom-call | tf_op jit(solution)/shard_map/pallas_call | solution.py:556
  3.2 4.6 %collective-permute-start.1 = (f32[4,32,128]{2,1,0:T(8,128)}, f32[4,32,128]{2,1,0:T(8,128)S(1)}, u32[]{:S(2)}, u32[]{:S(2)}) collective-permute-start(f32[4,32,128]{2,1,0:T(8,128)} %shard_map.68), channel_id=1, source_target_pairs={{1,2},{5,6},{9,10},{13,14},{17,18},{21,22},{25,26},{29,30},{33,34}... | collective-permute-start | bytes 196616 | tf_op jit(solution)/shard_map/ppermute | solution.py:575
  7.8 0.1 collective-permute-start
  8.0 0.1 pad_add_fusion.place
  8.0 2.0 %collective-permute-done.1.middle = f32[4,32,128]{2,1,0:T(8,128)S(1)} collective-permute-done((f32[4,32,128]{2,1,0:T(8,128)}, f32[4,32,128]{2,1,0:T(8,128)S(1)}, u32[]{:S(2)}, u32[]{:S(2)}) %collective-permute-start.1) | collective-permute-done | bytes 65568 | tf_op jit(solution)/shard_map/ppermute | solution.py:575
  10.0 0.0 collective-permute-done.pair
  10.0 0.0 copy-done
  10.0 2.3 %shard_map.69 = (f32[160,512]{1,0:T(8,128)S(1)}, f32[160,512]{1,0:T(8,128)S(1)}, f32[4,32,128]{2,1,0:T(8,128)S(1)}) custom-call(s32[3]{0:T(128)S(1)} %pad_add_fusion.place, f32[4,12,32,512]{3,2,1,0:T(8,128)} %states.7, f32[12,32,512]{2,1,0:T(8,128)} %cot.7, s32[32,512]{1,0:T(8,128)S(1)} %copy-done, f32[4,32,128]{2,1,0:T(8,128)S(1)} %collective-permute-done.pair, ...), custom_call_target="tpu_custom_call" | custom-call | tf_op jit(solution)/shard_map/pallas_call | solution.py:581
  12.3 1.3 %collective-permute-start.2 = (f32[160,512]{1,0:T(8,128)S(1)}, f32[160,512]{1,0:T(8,128)S(1)}, u32[]{:S(2)}, u32[]{:S(2)}) collective-permute-start(f32[160,512]{1,0:T(8,128)S(1)} %get-tuple-element.7), channel_id=1, source_target_pairs={{0,4},{4,8},{8,12},{12,16},{16,20},{20,24},{24,28},{28,32},{32,36}... | collective-permute-start | bytes 983048 | tf_op jit(solution)/shard_map/ppermute | solution.py:578
  13.6 9.2 %collective-permute-start.3 = (f32[160,512]{1,0:T(8,128)S(1)}, f32[160,512]{1,0:T(8,128)S(1)}, u32[]{:S(2)}, u32[]{:S(2)}) collective-permute-start(f32[160,512]{1,0:T(8,128)S(1)} %get-tuple-element.8), channel_id=1, source_target_pairs={{0,252},{4,0},{8,4},{12,8},{16,12},{20,16},{24,20},{28,24},{32,28}... | collective-permute-start | bytes 983048 | tf_op jit(solution)/shard_map/ppermute | solution.py:578
  22.8 0.0 copy-done.1
  22.8 0.0 copy-done.2
  22.8 8.9 %shard_map.70 = (f32[12,32,512]{2,1,0:T(8,128)}, f32[32,512]{1,0:T(8,128)}) custom-call(s32[3]{0:T(128)S(1)} %pad_add_fusion.place, f32[4]{0:T(128)S(1)} %copy-done.2, f32[4,12,32,512]{3,2,1,0:T(8,128)} %states.7, f32[12,32,512]{2,1,0:T(8,128)} %cot.7, s32[32,512]{1,0:T(8,128)S(1)} %copy-done, s32[32,512]{1,0:T(8,128)S(1)} %copy-done.1, ...), custom_call_target="tpu_custom_call" | custom-call | flops 160000000 | bytes 24000000 | tf_op jit(solution)/shard_map/pallas_call | solution.py:597
  31.7 0.0 collective-permute-done.2.from_west
  31.8 0.0 collective-permute-done.3.from_east
  31.8 7.1 %shard_map.71 = (f32[12,32,512]{2,1,0:T(8,128)}, f32[32,512]{1,0:T(8,128)}) custom-call(s32[3]{0:T(128)S(1)} %pad_add_fusion.place, f32[4]{0:T(128)S(1)} %copy-done.2, f32[4,12,32,512]{3,2,1,0:T(8,128)} %states.7, f32[12,32,512]{2,1,0:T(8,128)} %cot.7, s32[32,512]{1,0:T(8,128)S(1)} %copy-done, ...), custom_call_target="tpu_custom_call", output_to_operand_aliasing={{0}: (10, {}), {1}: (11, {})} | custom-call | tf_op jit(solution)/shard_map/pallas_call | solution.py:607
  (2 shorter events, 0.1 us)
Async XLA Ops:
  0.6 9.4 %copy-start = (s32[32,512]{1,0:T(8,128)S(1)}, s32[32,512]{1,0:T(8,128)}, u32[]{:S(2)}) copy-start(s32[32,512]{1,0:T(8,128)} %sea.7) | copy-start | bytes 196612
  0.6 22.2 %copy-start.1 = (s32[32,512]{1,0:T(8,128)S(1)}, s32[32,512]{1,0:T(8,128)}, u32[]{:S(2)}) copy-start(s32[32,512]{1,0:T(8,128)} %layer.3) | copy-start | bytes 196612
  0.7 22.2 %copy-start.2 = (f32[4]{0:T(128)S(1)}, f32[4]{0:T(128)}, u32[]{:S(2)}) copy-start(f32[4]{0:T(128)} %gravities.3) | copy-start | bytes 52
  3.2 6.7 %collective-permute-start.1 = (f32[4,32,128]{2,1,0:T(8,128)}, f32[4,32,128]{2,1,0:T(8,128)S(1)}, u32[]{:S(2)}, u32[]{:S(2)}) collective-permute-start(f32[4,32,128]{2,1,0:T(8,128)} %shard_map.68), channel_id=1, source_target_pairs={{1,2},{5,6},{9,10},{13,14},{17,18},{21,22},{25,26},{29,30},{33,34}... | collective-permute-start | bytes 196616 | tf_op jit(solution)/shard_map/ppermute | solution.py:575
  7.8 2.1 %collective-permute-start = (f32[4,32,128]{2,1,0:T(8,128)}, f32[4,32,128]{2,1,0:T(8,128)S(1)}, u32[]{:S(2)}, u32[]{:S(2)}) collective-permute-start(f32[4,32,128]{2,1,0:T(8,128)} %shard_map.68), channel_id=1, source_target_pairs={{0,1},{2,3},{4,5},{6,7},{8,9},{10,11},{12,13},{14,15},{16,17},{18,... | collective-permute-start | bytes 196616 | tf_op jit(solution)/shard_map/ppermute | solution.py:575
  12.3 19.4 %collective-permute-start.2 = (f32[160,512]{1,0:T(8,128)S(1)}, f32[160,512]{1,0:T(8,128)S(1)}, u32[]{:S(2)}, u32[]{:S(2)}) collective-permute-start(f32[160,512]{1,0:T(8,128)S(1)} %get-tuple-element.7), channel_id=1, source_target_pairs={{0,4},{4,8},{8,12},{12,16},{16,20},{20,24},{24,28},{28,32},{32,36}... | collective-permute-start | bytes 983048 | tf_op jit(solution)/shard_map/ppermute | solution.py:578
  13.6 18.2 %collective-permute-start.3 = (f32[160,512]{1,0:T(8,128)S(1)}, f32[160,512]{1,0:T(8,128)S(1)}, u32[]{:S(2)}, u32[]{:S(2)}) collective-permute-start(f32[160,512]{1,0:T(8,128)S(1)} %get-tuple-element.8), channel_id=1, source_target_pairs={{0,252},{4,0},{8,4},{12,8},{16,12},{20,16},{24,20},{28,24},{32,28}... | collective-permute-start | bytes 983048 | tf_op jit(solution)/shard_map/ppermute | solution.py:578

commit v3 on v2

--- a/solution.py
+++ b/solution.py
@@ -25,6 +25,11 @@
 f32 = jnp.float32
 
 
+def place_of():
+    lon, lat = lax.axis_index("lon"), lax.axis_index("lat")
+    return lat % 2, lat < lax.axis_size("lat") - 1, lat > 0, lon == 0
+
+
 def lanes(j):
     return slice(128 * j, 128 * j + 128)
 
@@ -38,11 +43,13 @@
 
 OFFSET = {}
 HALO = 0
-for _q in sorted(range(PLANES), key=lambda q: -depth(q)):
+for _q in sorted(range(SEA), key=lambda q: -depth(q)) + [SEA]:
     if depth(_q):
         OFFSET[_q] = HALO
         HALO += depth(_q)
 MESSAGE = HALO + N
+TAIL = MESSAGE - 8
+assert OFFSET[SEA] == TAIL
 
 
 def start(pairs, sems):
@@ -79,39 +86,33 @@
         strips[g] = total
 
 
-def row_pack_kernel(place, states, cot, sea, pair, middle, east, west, edge, top, bottom, flags, sems):
-    pairs = [(sea, flags)]
-    for buf, rows in ((top, slice(0, 8)), (bottom, slice(ROWS - 8, ROWS))):
+def row_pack_kernel(states, cot, east, west, top, bottom, sems):
+    pairs = []
+    for buf, rows in ((bottom, slice(ROWS - 8, ROWS)), (top, slice(0, 8))):
         pairs.append((states.at[:, :, rows, :], buf.at[:N]))
         pairs.append((cot.at[:, rows, :], buf.at[N]))
-    copies = start(pairs, sems)
+    wait(start(pairs, sems))
+    for q, row in OFFSET.items():
+        if q == SEA:
+            continue
+        d = depth(q)
+        east[row : row + d] = bottom[q // CH, q % CH, 8 - d :]
+        west[row : row + d] = top[q // CH, q % CH, :d]
+
+
+def attach_kernel(sea, pair, middle, east_in, west_in, edge, east, west, flags, tails, sems):
+    copies = start([(sea, flags)], sems)
+    odd = place_of()[0] == 1
     south = lax.broadcasted_iota(jnp.int32, (ROWS, 128), 1) % 8 < 4
     for g in range(GROUPS):
-        merged = jnp.where(south == (place[0] == 1), pair[g], middle[g])
+        merged = jnp.where(south == odd, pair[g], middle[g])
         edge[g] = merged
-        east[HALO:, lanes(g)] = merged[ROWS - N :]
-        west[HALO:, lanes(g)] = merged[:N]
+        tails[0, N:, lanes(g)] = merged[ROWS - N :]
+        tails[1, N:, lanes(g)] = merged[:N]
     wait(copies)
-    for q, row in OFFSET.items():
-        d = depth(q)
-        if q == SEA:
-            east[row : row + d] = flags[ROWS - d :].astype(f32)
-            west[row : row + d] = flags[:d].astype(f32)
-        else:
-            east[row : row + d] = bottom[q // CH, q % CH, 8 - d :]
-            west[row : row + d] = top[q // CH, q % CH, :d]
-
-
-def fill_halo(planes, message, first, last):
-    for q, row in OFFSET.items():
-        d = depth(q)
-        at = first if last is None else last - d
-        for j in range(W - 1):
-            planes[q, j, at : at + d, :] = message[row : row + d, lanes(j)]
-    at = first if last is None else last - N
-    for q in range(PLANES):
-        g, k = divmod(q, 16)
-        planes[q, W - 1, at : at + N, :] = pltpu.roll(message[HALO:, lanes(g)], (124 - 8 * k) % 128, 1)
+    tails[0, :N, :] = flags[ROWS - N :].astype(f32)
+    tails[1, :N, :] = flags[:N].astype(f32)
+    wait(start([(tails.at[0], east.at[TAIL:, :]), (tails.at[1], west.at[TAIL:, :])], sems))
 
 
 def fill_columns(planes, edge, blocks):
@@ -135,7 +136,7 @@
     ]
 
 
-def adjoint_steps(rows, arrive, place, gravities, spin, planes, picked, cur, nxt, mixed, acc):
+def adjoint_steps(rows, arrive, gravities, spin, planes, picked, cur, nxt, mixed, acc):
     T = rows // 8
     half = 0.5 * TIME_STEP
 
@@ -156,8 +157,9 @@
             cur[c, t] = value if c < L else value * sea_t
         acc[t] = jnp.zeros((8, CC), f32)
 
+    place = place_of()
     edge_lane = lax.broadcasted_iota(jnp.int32, (8, 128), 1)
-    inside = jnp.where(edge_lane < 64, place[1], place[2]) > 0
+    inside = (edge_lane < 64) & place[1] | (edge_lane >= 64) & place[2]
 
     def north(x):
         return pltpu.roll(x, CC - 1, 1)
@@ -266,8 +268,8 @@
 
 
 def main_kernel(
-    place,
-    gravities,
+    early,
+    gravities_in,
     states,
     cot,
     sea,
@@ -285,45 +287,54 @@
     flags,
     spins,
     edges,
+    gravities,
     sems,
     more,
 ):
-    blocks = [(0, 0, ROWS)]
-    first = start([(sea, flags), (edge, edges), (spin, spins)] + layer_copies(layer, picked, blocks), more)
-    copies = [own_copies(N, cot, planes, blocks, sems)]
-    for n in range(N - 1, -1, -1):
-        copies.append(own_copies(n, states.at[n], planes, blocks, sems))
-    for group in copies:
-        for copy in group:
-            copy.start()
-    wait(first)
-    for j in range(W - 1):
-        planes[SEA, j, :ROWS, :] = flags[:, lanes(j)].astype(f32)
-    fill_columns(planes, edges, blocks)
-    wait(copies[0])
-    adjoint_steps(
-        ROWS,
-        lambda n: wait(own_copies(n, states.at[n], planes, blocks, sems)),
-        place,
-        gravities,
-        spins,
-        planes,
-        picked,
-        cur,
-        nxt,
-        mixed,
-        acc,
-    )
-    pairs = []
-    for j in range(W - 1):
-        pairs.append((planes.at[COT : COT + CH, j, :ROWS, :], out.at[:, :, lanes(j)]))
-        pairs.append((planes.at[SEA, j, :ROWS, :], forcing.at[:, lanes(j)]))
-    wait(start(pairs, more))
+    @pl.when(place_of()[3] == early)
+    def _():
+        blocks = [(0, 0, ROWS)]
+        first = start([(gravities_in, gravities), (sea, flags), (edge, edges), (spin, spins)] + layer_copies(layer, picked, blocks), more)
+        copies = [own_copies(N, cot, planes, blocks, sems)]
+        for n in range(N - 1, -1, -1):
+            copies.append(own_copies(n, states.at[n], planes, blocks, sems))
+        for group in copies:
+            for copy in group:
+                copy.start()
+        wait(first)
+        for j in range(W - 1):
+            planes[SEA, j, :ROWS, :] = flags[:, lanes(j)].astype(f32)
+        fill_columns(planes, edges, blocks)
+        wait(copies[0])
+        adjoint_steps(
+            ROWS,
+            lambda n: wait(own_copies(n, states.at[n], planes, blocks, sems)),
+            gravities,
+            spins,
+            planes,
+            picked,
+            cur,
+            nxt,
+            mixed,
+            acc,
+        )
+        pairs = []
+        for j in range(W - 1):
+            pairs.append((planes.at[COT : COT + CH, j, :ROWS, :], out.at[:, :, lanes(j)]))
+            pairs.append((planes.at[SEA, j, :ROWS, :], forcing.at[:, lanes(j)]))
+        wait(start(pairs, more))
+
+
+def early_kernel(gravities, states, cot, sea, layer, spin, edge, west_in, out, forcing, west, *scratch):
+    main_kernel(True, gravities, states, cot, sea, layer, spin, edge, out, forcing, *scratch)
+
+
+def late_kernel(gravities, states, cot, sea, layer, spin, edge, out_in, forcing_in, out, forcing, *scratch):
+    main_kernel(False, gravities, states, cot, sea, layer, spin, edge, out, forcing, *scratch)
 
 
 def rim_kernel(
-    place,
-    gravities,
+    gravities_in,
     states,
     cot,
     sea,
@@ -350,22 +361,29 @@
     wests,
     easts,
     tiles,
+    gravities,
     sems,
     more,
 ):
-    first = start([(from_west, wests), (from_east, easts), (edge, edges), (sea, flags), (layer, layers), (spin, spins)], more)
+    first = start([(from_west, wests), (from_east, easts), (edge, edges), (sea, flags), (layer, layers), (spin, spins), (gravities_in, gravities)], more)
     copies = {}
-    for n in range(N, -1, -1):
+
+    def fetch(n):
         source = cot if n == N else states.at[n]
         copies[n] = start(
             [(source.at[:, :8, :], own.at[n, 0]), (source.at[:, ROWS - 8 :, :], own.at[n, 1])], sems.at[n]
         )
+
+    fetch(N)
+    fetch(N - 1)
+    wait(first)
+    for n in range(N - 2, -1, -1):
+        fetch(n)
     back = []
     for e, row in enumerate((0, ROWS - 8)):
         back.append((out_in.at[:, row : row + 8, :], tiles.at[e, :CH]))
         back.append((forcing_in.at[row : row + 8, :], tiles.at[e, CH]))
-    back = start(back, more.at[6:])
-    wait(first)
+    back = start(back, more.at[7:])
 
     def put(target, at, q, e, s):
         g, k = divmod(q, 16)
@@ -411,8 +429,9 @@
             weight = jnp.where(level == k, half * sums[min(k, (k - m) % L)], weight)
         couple.append(weight)
     keep = jnp.where(level == L - 1, 1.0 - TIME_STEP * (4.0 * VISCOSITY + BOTTOM_DRAG), 1.0 - TIME_STEP * 4.0 * VISCOSITY)
+    place = place_of()
     edge_lane = lax.broadcasted_iota(jnp.int32, (8, 128), 1)
-    inside = jnp.where(edge_lane < 64, place[1], place[2]) > 0
+    inside = (edge_lane < 64) & place[1] | (edge_lane >= 64) & place[2]
 
     def row(ref, at, r):
         return jnp.concatenate([ref[at, j, pl.ds(pl.multiple_of(8 * r, 8), 8), :] for j in range(W)], axis=1)
@@ -521,7 +540,6 @@
 
 
 VMEM = pl.BlockSpec(memory_space=pltpu.VMEM)
-SMEM = pl.BlockSpec(memory_space=pltpu.SMEM)
 ANY = pl.BlockSpec(memory_space=pl.ANY)
 HBM = pl.BlockSpec(memory_space=pltpu.HBM)
 DMA = pltpu.SemaphoreType.DMA
@@ -551,8 +569,6 @@
     lat_rows = (lat * COLS + lane).astype(f32)
     spin = 2.0 * jnp.sin(jnp.pi * ((lat_rows + 0.5) / (lats * COLS) - 0.5))
     spin = jnp.broadcast_to(spin[None], (8, CC))
-    place = jnp.stack([lat % 2, (lat < lats - 1).astype(jnp.int32), (lat > 0).astype(jnp.int32)])
-
     strips = pl.pallas_call(
         strip_pack_kernel,
         out_shape=shape((GROUPS, ROWS, 128), f32),
@@ -578,36 +594,59 @@
         return lax.ppermute(x, "lon", [(i, (i + by) % lons) for i in range(lons)])
 
     pair, middle = swap(strips, 0), swap(strips, 1)
-    east, west, edge = pl.pallas_call(
+    east, west = pl.pallas_call(
         row_pack_kernel,
-        out_shape=[shape((MESSAGE, COLS), f32), shape((MESSAGE, COLS), f32), shape((GROUPS, ROWS, 128), f32)],
-        in_specs=[SMEM, HBM, HBM, HBM, VMEM, VMEM],
-        out_specs=[VMEM] * 3,
+        out_shape=[shape((MESSAGE, COLS), f32)] * 2,
+        in_specs=[HBM] * 2,
+        out_specs=[VMEM] * 2,
         scratch_shapes=[
             pltpu.VMEM((N + 1, CH, 8, COLS), f32),
             pltpu.VMEM((N + 1, CH, 8, COLS), f32),
-            pltpu.VMEM((ROWS, COLS), jnp.int32),
-            DMA((5,)),
+            DMA((4,)),
         ],
         compiler_params=pltpu.CompilerParams(vmem_limit_bytes=53 << 20),
-    )(place, saved_states, final_cotangent, sea_mask, pair, middle)
-    from_west, from_east = shift(east, 1), shift(west, -1)
+    )(saved_states, final_cotangent)
+    edge, east, west = pl.pallas_call(
+        attach_kernel,
+        out_shape=[shape((GROUPS, ROWS, 128), f32)] + [shape((MESSAGE, COLS), f32)] * 2,
+        in_specs=[HBM, VMEM, VMEM, HBM, HBM],
+        out_specs=[VMEM, HBM, HBM],
+        scratch_shapes=[pltpu.VMEM((ROWS, COLS), jnp.int32), pltpu.VMEM((2, 8, COLS), f32), DMA((2,))],
+        input_output_aliases={3: 1, 4: 2},
+        compiler_params=pltpu.CompilerParams(vmem_limit_bytes=53 << 20),
+    )(sea_mask, pair, middle, east, west)
 
     outs = [shape((CH, ROWS, COLS), f32), shape((ROWS, COLS), f32)]
-    out, forcing = pl.pallas_call(
-        main_kernel,
-        out_shape=outs,
-        in_specs=[SMEM, SMEM] + [HBM] * 4 + [ANY] * 2,
-        out_specs=[HBM, HBM],
-        scratch_shapes=ring_scratch(ROWS) + [DMA((N + 1, W - 1, 1)), DMA((16,))],
+    main = dict(
+        scratch_shapes=ring_scratch(ROWS) + [pltpu.SMEM((L,), f32), DMA((N + 1, W - 1, 1)), DMA((16,))],
         compiler_params=pltpu.CompilerParams(vmem_limit_bytes=53 << 20),
         cost_estimate=pl.CostEstimate(flops=160_000_000, bytes_accessed=24_000_000, transcendentals=0),
-    )(place, gravities, saved_states, final_cotangent, sea_mask, layer_index, spin, edge)
+    )
+    fixed = (gravities, saved_states, final_cotangent, sea_mask, layer_index, spin, edge)
+    specs = [ANY] + [HBM] * 4 + [ANY] * 2
+    from_west = shift(east, 1)
+    out, forcing, west = pl.pallas_call(
+        early_kernel,
+        out_shape=outs + [shape((MESSAGE, COLS), f32)],
+        in_specs=specs + [HBM],
+        out_specs=[HBM] * 3,
+        input_output_aliases={7: 2},
+        **main,
+    )(*fixed, west)
+    from_east = shift(west, -1)
+    out, forcing = pl.pallas_call(
+        late_kernel,
+        out_shape=outs,
+        in_specs=specs + [HBM] * 2,
+        out_specs=[HBM] * 2,
+        input_output_aliases={7: 0, 8: 1},
+        **main,
+    )(*fixed, out, forcing)
 
     return pl.pallas_call(
         rim_kernel,
         out_shape=outs,
-        in_specs=[SMEM, SMEM] + [HBM] * 4 + [ANY] * 4 + [HBM] * 2,
+        in_specs=[ANY] + [HBM] * 4 + [ANY] * 4 + [HBM] * 2,
         out_specs=[HBM, HBM],
         scratch_shapes=[
             pltpu.VMEM((N + 1, 2, CH, 8, COLS), f32),
@@ -624,13 +663,13 @@
             pltpu.VMEM((MESSAGE, COLS), f32),
             pltpu.VMEM((MESSAGE, COLS), f32),
             pltpu.VMEM((2, CH + 1, 8, COLS), f32),
+            pltpu.SMEM((L,), f32),
             DMA((N + 1, 2)),
-            DMA((10,)),
+            DMA((11,)),
         ],
-        input_output_aliases={10: 0, 11: 1},
+        input_output_aliases={9: 0, 10: 1},
         compiler_params=pltpu.CompilerParams(vmem_limit_bytes=53 << 20),
     )(
-        place,
         gravities,
         saved_states,
         final_cotangent,

time: 39 us -> 35.6 us (0.913)
  starting transfers between devices: 15.1 us -> 7.25 us
  waiting for transfers between devices: 1.96 us -> 7.71 us
  Pallas kernels: 20.9 us -> 19.6 us
    ppermute x2, starting transfers between devices: 10.4 us -> 2.43 us  [shift(): return lax.ppermute(x, 'lon', [(i, (i + by) % lons) for i in range(lons)])]
    ppermute x2, waiting for transfers between devices: 0.01 us -> 7.39 us  [shift(): return lax.ppermute(x, 'lon', [(i, (i + by) % lons) for i in range(lons)])]
    ppermute x2, waiting for transfers between devices: 1.96 us -> 0.31 us  [swap(): return lax.ppermute(x, ('lon', 'lat'), pairs + [(b, a) for a, b in pairs])]
    pallas_call x3 -> x5, Pallas kernels: 18.3 us -> 17.1 us  [the longest x1 8.38 us: per_device(): pl.pallas_call(early_kernel, out_shape=outs + [shape((MESSAGE, COLS), f32...]
  transfers between devices with their start and end apart: 4 -> 4, of which waited for: 1 -> 3; matrix products, arithmetic and copies ran while one was open for 0% -> 0% of each run, Pallas kernels for 23% -> 29%
where the time goes in v3:
time: 35.6 us; the launch traced here: 35.4 us
  Pallas kernels  19.6 us (55%)
  waiting for transfers between devices  7.71 us (22%)
  starting transfers between devices  7.25 us (20%)
  between operations  0.72 us (2%)
    pallas_call x1, Pallas kernels, per_device(): pl.pallas_call(early_kernel, out_shape=outs + [shape((MESSAGE, COLS), f32...  8.38 us
    ppermute x2, waiting for transfers between devices, shift(): return lax.ppermute(x, 'lon', [(i, (i + by) % lons) for i in range(lons)])  7.39 us
    pallas_call x1, Pallas kernels, per_device(): pl.pallas_call(rim_kernel, out_shape=outs, in_specs=[ANY] + [HBM] * 4 + [...  6.54 us
    ppermute x2, starting transfers between devices, swap(): return lax.ppermute(x, ('lon', 'lat'), pairs + [(b, a) for a, b in pairs])  4.82 us
    pallas_call x1, Pallas kernels, per_device(): pl.pallas_call(strip_pack_kernel, out_shape=shape((GROUPS, ROWS, 128), f3...  2.55 us
    ppermute x2, starting transfers between devices, shift(): return lax.ppermute(x, 'lon', [(i, (i + by) % lons) for i in range(lons)])  2.43 us
    pallas_call x1, Pallas kernels, per_device(): pl.pallas_call(row_pack_kernel, out_shape=[shape((MESSAGE, COLS), f32)] *...  1.67 us
  transfers between devices with their start and end apart: 4, of which 3 were waited for; matrix products, arithmetic and copies ran while one was open for 0% of the time, Pallas kernels for 29%

profile of v3, /device:TPU:1, one launch (start us, length us, event | category | flops | bytes accessed | tf_op | source)
XLA Modules:
  0.0 35.4 jit_solution(9768895908069003899)
XLA Ops:
  0.6 0.0 copy-start
  0.6 2.6 %shard_map.68 = f32[4,32,128]{2,1,0:T(8,128)} custom-call(f32[4,12,32,512]{3,2,1,0:T(8,128)} %states.9, f32[12,32,512]{2,1,0:T(8,128)} %cot.9, s32[32,512]{1,0:T(8,128)} %sea.9), custom_call_target="tpu_custom_call" | custom-call | tf_op jit(solution)/shard_map/pallas_call | solution.py:572
  3.2 0.0 copy-start.1
  3.2 0.0 copy-start.2
  3.2 4.7 %collective-permute-start.1 = (f32[4,32,128]{2,1,0:T(8,128)}, f32[4,32,128]{2,1,0:T(8,128)S(1)}, u32[]{:S(2)}, u32[]{:S(2)}) collective-permute-start(f32[4,32,128]{2,1,0:T(8,128)} %shard_map.68), channel_id=1, source_target_pairs={{1,2},{5,6},{9,10},{13,14},{17,18},{21,22},{25,26},{29,30},{33,34}... | collective-permute-start | bytes 196616 | tf_op jit(solution)/shard_map/ppermute | solution.py:591
  8.0 0.1 collective-permute-start
  8.1 1.7 %shard_map.69 = (f32[160,512]{1,0:T(8,128)S(1)}, f32[160,512]{1,0:T(8,128)S(1)}) custom-call(f32[4,12,32,512]{3,2,1,0:T(8,128)} %states.9, f32[12,32,512]{2,1,0:T(8,128)} %cot.9), custom_call_target="tpu_custom_call" | custom-call | tf_op jit(solution)/shard_map/pallas_call | solution.py:597
  9.8 0.3 collective-permute-done.1.middle
  10.1 0.0 collective-permute-done.pair
  10.1 0.0 copy-done
  10.1 0.2 shard_map.70
  10.3 1.3 %collective-permute-start.2 = (f32[160,512]{1,0:T(8,128)S(1)}, f32[160,512]{1,0:T(8,128)S(1)}, u32[]{:S(2)}, u32[]{:S(2)}) collective-permute-start(f32[160,512]{1,0:T(8,128)S(1)} %get-tuple-element.14), channel_id=1, source_target_pairs={{0,4},{4,8},{8,12},{12,16},{16,20},{20,24},{24,28},{28,32},{32,36}... | collective-permute-start | bytes 983048 | tf_op jit(solution)/shard_map/ppermute | solution.py:594
  11.6 0.0 copy-done.1
  11.6 0.0 copy-done.2
  11.6 8.4 %shard_map.71 = (f32[12,32,512]{2,1,0:T(8,128)}, f32[32,512]{1,0:T(8,128)}, f32[160,512]{1,0:T(8,128)S(1)}) custom-call(f32[4]{0:T(128)S(1)} %copy-done.2, f32[4,12,32,512]{3,2,1,0:T(8,128)} %states.9, f32[12,32,512]{2,1,0:T(8,128)} %cot.9, s32[32,512]{1,0:T(8,128)S(1)} %copy-done, s32[32,512]{1,0:T(8,128)S(1)} %copy-done.1, ...), custom_call_target="tpu_custom_call", output_to_operand_aliasing={{2}: (7, {})} | custom-call | flops 160000000 | bytes 24000000 | tf_op jit(solution)/shard_map/pallas_call | solution.py:628
  20.0 1.1 %collective-permute-start.3 = (f32[160,512]{1,0:T(8,128)S(1)}, f32[160,512]{1,0:T(8,128)S(1)}, u32[]{:S(2)}, u32[]{:S(2)}) collective-permute-start(f32[160,512]{1,0:T(8,128)S(1)} %get-tuple-element.17), channel_id=1, source_target_pairs={{0,252},{4,0},{8,4},{12,8},{16,12},{20,16},{24,20},{28,24},{32,28}... | collective-permute-start | bytes 983048 | tf_op jit(solution)/shard_map/ppermute | solution.py:594
  21.1 0.3 shard_map.72
  21.4 7.2 %collective-permute-done.2.from_west = f32[160,512]{1,0:T(8,128)S(1)} collective-permute-done((f32[160,512]{1,0:T(8,128)S(1)}, f32[160,512]{1,0:T(8,128)S(1)}, u32[]{:S(2)}, u32[]{:S(2)}) %collective-permute-start.2) | collective-permute-done | bytes 327712 | tf_op jit(solution)/shard_map/ppermute | solution.py:594
  28.7 0.1 collective-permute-done.3.from_east
  28.8 6.5 %shard_map.73 = (f32[12,32,512]{2,1,0:T(8,128)}, f32[32,512]{1,0:T(8,128)}) custom-call(f32[4]{0:T(128)S(1)} %copy-done.2, f32[4,12,32,512]{3,2,1,0:T(8,128)} %states.9, f32[12,32,512]{2,1,0:T(8,128)} %cot.9, s32[32,512]{1,0:T(8,128)S(1)} %copy-done, s32[32,512]{1,0:T(8,128)S(1)} %copy-done.1, ...), custom_call_target="tpu_custom_call", output_to_operand_aliasing={{0}: (9, {}), {1}: (10, {})} | custom-call | tf_op jit(solution)/shard_map/pallas_call | solution.py:646
  (2 shorter events, 0.1 us)
Async XLA Ops:
  0.6 9.5 %copy-start = (s32[32,512]{1,0:T(8,128)S(1)}, s32[32,512]{1,0:T(8,128)}, u32[]{:S(2)}) copy-start(s32[32,512]{1,0:T(8,128)} %sea.9) | copy-start | bytes 196612
  3.2 8.4 %copy-start.1 = (s32[32,512]{1,0:T(8,128)S(1)}, s32[32,512]{1,0:T(8,128)}, u32[]{:S(2)}) copy-start(s32[32,512]{1,0:T(8,128)} %layer.5) | copy-start | bytes 196612
  3.2 8.4 %copy-start.2 = (f32[4]{0:T(128)S(1)}, f32[4]{0:T(128)}, u32[]{:S(2)}) copy-start(f32[4]{0:T(128)} %gravities_in.1) | copy-start | bytes 52
  3.2 6.9 %collective-permute-start.1 = (f32[4,32,128]{2,1,0:T(8,128)}, f32[4,32,128]{2,1,0:T(8,128)S(1)}, u32[]{:S(2)}, u32[]{:S(2)}) collective-permute-start(f32[4,32,128]{2,1,0:T(8,128)} %shard_map.68), channel_id=1, source_target_pairs={{1,2},{5,6},{9,10},{13,14},{17,18},{21,22},{25,26},{29,30},{33,34}... | collective-permute-start | bytes 196616 | tf_op jit(solution)/shard_map/ppermute | solution.py:591
  8.0 2.1 %collective-permute-start = (f32[4,32,128]{2,1,0:T(8,128)}, f32[4,32,128]{2,1,0:T(8,128)S(1)}, u32[]{:S(2)}, u32[]{:S(2)}) collective-permute-start(f32[4,32,128]{2,1,0:T(8,128)} %shard_map.68), channel_id=1, source_target_pairs={{0,1},{2,3},{4,5},{6,7},{8,9},{10,11},{12,13},{14,15},{16,17},{18,... | collective-permute-start | bytes 196616 | tf_op jit(solution)/shard_map/ppermute | solution.py:591
  10.3 18.4 %collective-permute-start.2 = (f32[160,512]{1,0:T(8,128)S(1)}, f32[160,512]{1,0:T(8,128)S(1)}, u32[]{:S(2)}, u32[]{:S(2)}) collective-permute-start(f32[160,512]{1,0:T(8,128)S(1)} %get-tuple-element.14), channel_id=1, source_target_pairs={{0,4},{4,8},{8,12},{12,16},{16,20},{20,24},{24,28},{28,32},{32,36}... | collective-permute-start | bytes 983048 | tf_op jit(solution)/shard_map/ppermute | solution.py:594
  20.0 8.9 %collective-permute-start.3 = (f32[160,512]{1,0:T(8,128)S(1)}, f32[160,512]{1,0:T(8,128)S(1)}, u32[]{:S(2)}, u32[]{:S(2)}) collective-permute-start(f32[160,512]{1,0:T(8,128)S(1)} %get-tuple-element.17), channel_id=1, source_target_pairs={{0,252},{4,0},{8,4},{12,8},{16,12},{20,16},{24,20},{28,24},{32,28}... | collective-permute-start | bytes 983048 | tf_op jit(solution)/shard_map/ppermute | solution.py:594

commit v4 on v3

--- a/solution.py
+++ b/solution.py
@@ -86,18 +86,18 @@
         strips[g] = total
 
 
-def row_pack_kernel(states, cot, east, west, top, bottom, sems):
+def row_pack_kernel(states, cot, east, west, own, sems):
     pairs = []
-    for buf, rows in ((bottom, slice(ROWS - 8, ROWS)), (top, slice(0, 8))):
-        pairs.append((states.at[:, :, rows, :], buf.at[:N]))
-        pairs.append((cot.at[:, rows, :], buf.at[N]))
+    for e, rows in enumerate((slice(0, 8), slice(ROWS - 8, ROWS))):
+        pairs.append((states.at[:, :, rows, :], own.at[e, :N]))
+        pairs.append((cot.at[:, rows, :], own.at[e, N]))
     wait(start(pairs, sems))
     for q, row in OFFSET.items():
         if q == SEA:
             continue
         d = depth(q)
-        east[row : row + d] = bottom[q // CH, q % CH, 8 - d :]
-        west[row : row + d] = top[q // CH, q % CH, :d]
+        east[row : row + d] = own[1, q // CH, q % CH, 8 - d :]
+        west[row : row + d] = own[0, q // CH, q % CH, :d]
 
 
 def attach_kernel(sea, pair, middle, east_in, west_in, edge, east, west, flags, tails, sems):
@@ -335,8 +335,7 @@
 
 def rim_kernel(
     gravities_in,
-    states,
-    cot,
+    own,
     sea,
     layer,
     spin,
@@ -347,7 +346,6 @@
     forcing_in,
     out,
     forcing,
-    own,
     fields,
     cur,
     nxt,
@@ -357,65 +355,48 @@
     flags,
     layers,
     spins,
-    edges,
-    wests,
-    easts,
     tiles,
     gravities,
-    sems,
     more,
 ):
-    first = start([(from_west, wests), (from_east, easts), (edge, edges), (sea, flags), (layer, layers), (spin, spins), (gravities_in, gravities)], more)
-    copies = {}
-
-    def fetch(n):
-        source = cot if n == N else states.at[n]
-        copies[n] = start(
-            [(source.at[:, :8, :], own.at[n, 0]), (source.at[:, ROWS - 8 :, :], own.at[n, 1])], sems.at[n]
-        )
-
-    fetch(N)
-    fetch(N - 1)
-    wait(first)
-    for n in range(N - 2, -1, -1):
-        fetch(n)
+    first = start([(sea, flags), (layer, layers), (spin, spins), (gravities_in, gravities)], more)
     back = []
     for e, row in enumerate((0, ROWS - 8)):
         back.append((out_in.at[:, row : row + 8, :], tiles.at[e, :CH]))
         back.append((forcing_in.at[row : row + 8, :], tiles.at[e, CH]))
-    back = start(back, more.at[7:])
+    back = start(back, more.at[4:])
 
     def put(target, at, q, e, s):
         g, k = divmod(q, 16)
         d = depth(q)
         tile = slice(0, 8) if e == 0 else slice(ROWS - 8, ROWS)
-        message = (wests, easts)[e]
+        message = (from_west, from_east)[e]
         here = 4 if e == 0 else 0
         halo = 4 - d if e == 0 else 8
         for j in range(W - 1):
             if q == SEA:
                 value = flags[tile, lanes(j)].astype(f32)
             else:
-                value = own[q // CH, e, q % CH, :, lanes(j)]
+                value = own[e, q // CH, q % CH, :, lanes(j)]
             target[at, j, pl.ds(8 * here + s, 8, stride=8), :] = value
             if d:
                 value = message[OFFSET[q] : OFFSET[q] + d, lanes(j)]
                 target[at, j, pl.ds(8 * halo + s, d, stride=8), :] = value
         shift = (124 - 8 * k) % 128
-        target[at, W - 1, pl.ds(8 * here + s, 8, stride=8), :] = pltpu.roll(edges[g, tile, :], shift, 1)
+        target[at, W - 1, pl.ds(8 * here + s, 8, stride=8), :] = pltpu.roll(edge[g, tile, :], shift, 1)
         corner = pltpu.roll(message[HALO:, lanes(g)], shift, 1)
         target[at, W - 1, pl.ds(8 * (0 if e == 0 else 8) + s, 4, stride=8), :] = corner
 
+    for e in range(2):
+        for c in range(CH):
+            put(cur, c // L, COT + c, e, 2 * (c % L) + e)
+    wait(first)
     for e in range(2):
         for k in range(L):
             put(mask, 0, SEA, e, 2 * k + e)
             for j in range(W - 1):
                 tile = slice(0, 4) if e == 0 else slice(ROWS - 4, ROWS)
                 picked[j, pl.ds(2 * k + e, 4, stride=8), :] = layers[tile, lanes(j)]
-    wait(copies[N])
-    for e in range(2):
-        for c in range(CH):
-            put(cur, c // L, COT + c, e, 2 * (c % L) + e)
 
     half = 0.5 * TIME_STEP
     level = lax.broadcasted_iota(jnp.int32, (8, CC), 0) // 2
@@ -456,7 +437,6 @@
     for i in range(N):
         n = N - 1 - i
         src, dst = (cur, nxt) if i % 2 == 0 else (nxt, cur)
-        wait(copies[n])
         for e in range(2):
             for c in range(CH):
                 put(fields, c // L, n * CH + c, e, 2 * (c % L) + e)
@@ -594,17 +574,13 @@
         return lax.ppermute(x, "lon", [(i, (i + by) % lons) for i in range(lons)])
 
     pair, middle = swap(strips, 0), swap(strips, 1)
-    east, west = pl.pallas_call(
+    east, west, own = pl.pallas_call(
         row_pack_kernel,
-        out_shape=[shape((MESSAGE, COLS), f32)] * 2,
+        out_shape=[shape((MESSAGE, COLS), f32)] * 2 + [shape((2, N + 1, CH, 8, COLS), f32)],
         in_specs=[HBM] * 2,
-        out_specs=[VMEM] * 2,
-        scratch_shapes=[
-            pltpu.VMEM((N + 1, CH, 8, COLS), f32),
-            pltpu.VMEM((N + 1, CH, 8, COLS), f32),
-            DMA((4,)),
-        ],
-        compiler_params=pltpu.CompilerParams(vmem_limit_bytes=53 << 20),
+        out_specs=[VMEM] * 3,
+        scratch_shapes=[DMA((4,))],
+        compiler_params=pltpu.CompilerParams(vmem_limit_bytes=51 << 20),
     )(saved_states, final_cotangent)
     edge, east, west = pl.pallas_call(
         attach_kernel,
@@ -613,13 +589,13 @@
         out_specs=[VMEM, HBM, HBM],
         scratch_shapes=[pltpu.VMEM((ROWS, COLS), jnp.int32), pltpu.VMEM((2, 8, COLS), f32), DMA((2,))],
         input_output_aliases={3: 1, 4: 2},
-        compiler_params=pltpu.CompilerParams(vmem_limit_bytes=53 << 20),
+        compiler_params=pltpu.CompilerParams(vmem_limit_bytes=51 << 20),
     )(sea_mask, pair, middle, east, west)
 
     outs = [shape((CH, ROWS, COLS), f32), shape((ROWS, COLS), f32)]
     main = dict(
         scratch_shapes=ring_scratch(ROWS) + [pltpu.SMEM((L,), f32), DMA((N + 1, W - 1, 1)), DMA((16,))],
-        compiler_params=pltpu.CompilerParams(vmem_limit_bytes=53 << 20),
+        compiler_params=pltpu.CompilerParams(vmem_limit_bytes=51 << 20),
         cost_estimate=pl.CostEstimate(flops=160_000_000, bytes_accessed=24_000_000, transcendentals=0),
     )
     fixed = (gravities, saved_states, final_cotangent, sea_mask, layer_index, spin, edge)
@@ -646,10 +622,9 @@
     return pl.pallas_call(
         rim_kernel,
         out_shape=outs,
-        in_specs=[ANY] + [HBM] * 4 + [ANY] * 4 + [HBM] * 2,
+        in_specs=[ANY, VMEM, ANY, ANY, ANY] + [VMEM] * 3 + [HBM] * 2,
         out_specs=[HBM, HBM],
         scratch_shapes=[
-            pltpu.VMEM((N + 1, 2, CH, 8, COLS), f32),
             pltpu.VMEM((3, W, 96, 128), f32),
             pltpu.VMEM((3, W, 96, 128), f32),
             pltpu.VMEM((3, W, 96, 128), f32),
@@ -659,20 +634,15 @@
             pltpu.VMEM((ROWS, COLS), jnp.int32),
             pltpu.VMEM((ROWS, COLS), jnp.int32),
             pltpu.VMEM((8, CC), f32),
-            pltpu.VMEM((GROUPS, ROWS, 128), f32),
-            pltpu.VMEM((MESSAGE, COLS), f32),
-            pltpu.VMEM((MESSAGE, COLS), f32),
             pltpu.VMEM((2, CH + 1, 8, COLS), f32),
             pltpu.SMEM((L,), f32),
-            DMA((N + 1, 2)),
-            DMA((11,)),
+            DMA((8,)),
         ],
-        input_output_aliases={9: 0, 10: 1},
-        compiler_params=pltpu.CompilerParams(vmem_limit_bytes=53 << 20),
+        input_output_aliases={8: 0, 9: 1},
+        compiler_params=pltpu.CompilerParams(vmem_limit_bytes=51 << 20),
     )(
         gravities,
-        saved_states,
-        final_cotangent,
+        own,
         sea_mask,
         layer_index,
         spin,

time: 35.6 us -> 34.5 us (0.969)
  waiting for transfers between devices: 7.71 us -> 7.12 us
  Pallas kernels: 19.6 us -> 19.2 us
    pallas_call x1, Pallas kernels: 6.54 us -> 5.12 us  [per_device(): pl.pallas_call(rim_kernel, out_shape=outs, in_specs=[ANY, VMEM, ANY, ANY,...]
    pallas_call x1, Pallas kernels: 1.67 us -> 2.71 us  [per_device(): pl.pallas_call(row_pack_kernel, out_shape=[shape((MESSAGE, COLS), f32)] *...]
  transfers between devices with their start and end apart: 4 -> 4, of which waited for: 3 -> 2; matrix products, arithmetic and copies ran while one was open for 0% -> 0% of each run, Pallas kernels for 29% -> 33%
where the time goes in v4:
time: 34.5 us; the launch traced here: 34.3 us
  Pallas kernels  19.2 us (56%)
  starting transfers between devices  7.22 us (21%)
  waiting for transfers between devices  7.12 us (21%)
  between operations  0.77 us (2%)
    pallas_call x1, Pallas kernels, per_device(): pl.pallas_call(early_kernel, out_shape=outs + [shape((MESSAGE, COLS), f32...  8.23 us
    ppermute x2, waiting for transfers between devices, shift(): return lax.ppermute(x, 'lon', [(i, (i + by) % lons) for i in range(lons)])  7.11 us
    pallas_call x1, Pallas kernels, per_device(): pl.pallas_call(rim_kernel, out_shape=outs, in_specs=[ANY, VMEM, ANY, ANY,...  5.12 us
    ppermute x2, starting transfers between devices, swap(): return lax.ppermute(x, ('lon', 'lat'), pairs + [(b, a) for a, b in pairs])  4.82 us
    pallas_call x1, Pallas kernels, per_device(): pl.pallas_call(row_pack_kernel, out_shape=[shape((MESSAGE, COLS), f32)] *...  2.71 us
    pallas_call x1, Pallas kernels, per_device(): pl.pallas_call(strip_pack_kernel, out_shape=shape((GROUPS, ROWS, 128), f3...  2.6 us
    ppermute x2, starting transfers between devices, shift(): return lax.ppermute(x, 'lon', [(i, (i + by) % lons) for i in range(lons)])  2.4 us
  transfers between devices with their start and end apart: 4, of which 2 were waited for; matrix products, arithmetic and copies ran while one was open for 0% of the time, Pallas kernels for 33%

profile of v4, /device:TPU:1, one launch (start us, length us, event | category | flops | bytes accessed | tf_op | source)
XLA Modules:
  0.0 34.3 jit_solution(12845204273890561555)
XLA Ops:
  0.6 0.0 copy-start.2
  0.6 0.0 copy-start
  0.6 2.6 %shard_map.69 = f32[4,32,128]{2,1,0:T(8,128)} custom-call(f32[4,12,32,512]{3,2,1,0:T(8,128)} %states.7, f32[12,32,512]{2,1,0:T(8,128)} %cot.7, s32[32,512]{1,0:T(8,128)} %sea.9), custom_call_target="tpu_custom_call" | custom-call | tf_op jit(solution)/shard_map/pallas_call | solution.py:552
  3.3 0.0 copy-start.3
  3.3 0.0 copy-start.4
  3.3 4.7 %collective-permute-start.1 = (f32[4,32,128]{2,1,0:T(8,128)}, f32[4,32,128]{2,1,0:T(8,128)S(1)}, u32[]{:S(2)}, u32[]{:S(2)}) collective-permute-start(f32[4,32,128]{2,1,0:T(8,128)} %shard_map.69), channel_id=1, source_target_pairs={{1,2},{5,6},{9,10},{13,14},{17,18},{21,22},{25,26},{29,30},{33,34}... | collective-permute-start | bytes 196616 | tf_op jit(solution)/shard_map/ppermute | solution.py:571
  8.0 0.1 collective-permute-start
  8.1 0.0 copy-done
  8.1 2.7 %shard_map.68 = (f32[160,512]{1,0:T(8,128)S(1)}, f32[160,512]{1,0:T(8,128)S(1)}, f32[2,5,12,8,512]{4,3,2,1,0:T(8,128)}) custom-call(f32[4,12,32,512]{3,2,1,0:T(8,128)} %states.7, f32[12,32,512]{2,1,0:T(8,128)S(1)} %copy-done), custom_call_target="tpu_custom_call" | custom-call | tf_op jit(solution)/shard_map/pallas_call | solution.py:577
  10.9 0.0 collective-permute-done.1.middle
  10.9 0.0 collective-permute-done.pair
  10.9 0.0 copy-done.2
  10.9 0.2 shard_map.70
  11.1 1.3 %collective-permute-start.2 = (f32[160,512]{1,0:T(8,128)S(1)}, f32[160,512]{1,0:T(8,128)S(1)}, u32[]{:S(2)}, u32[]{:S(2)}) collective-permute-start(f32[160,512]{1,0:T(8,128)S(1)} %get-tuple-element.16), channel_id=1, source_target_pairs={{0,4},{4,8},{8,12},{12,16},{16,20},{20,24},{24,28},{28,32},{32,36}... | collective-permute-start | bytes 983048 | tf_op jit(solution)/shard_map/ppermute | solution.py:574
  12.4 0.0 copy-done.3
  12.4 0.0 copy-done.4
  12.4 8.2 %shard_map.71 = (f32[12,32,512]{2,1,0:T(8,128)}, f32[32,512]{1,0:T(8,128)}, f32[160,512]{1,0:T(8,128)S(1)}) custom-call(f32[4]{0:T(128)S(1)} %copy-done.4, f32[4,12,32,512]{3,2,1,0:T(8,128)} %states.7, f32[12,32,512]{2,1,0:T(8,128)S(1)} %copy-done, s32[32,512]{1,0:T(8,128)S(1)} %copy-done.2, ...), custom_call_target="tpu_custom_call", output_to_operand_aliasing={{2}: (7, {})} | custom-call | flops 160000000 | bytes 24000000 | tf_op jit(solution)/shard_map/pallas_call | solution.py:604
  20.6 0.0 copy-start.1
  20.7 1.1 %collective-permute-start.3 = (f32[160,512]{1,0:T(8,128)S(1)}, f32[160,512]{1,0:T(8,128)S(1)}, u32[]{:S(2)}, u32[]{:S(2)}) collective-permute-start(f32[160,512]{1,0:T(8,128)S(1)} %get-tuple-element.19), channel_id=1, source_target_pairs={{0,252},{4,0},{8,4},{12,8},{16,12},{20,16},{24,20},{28,24},{32,28}... | collective-permute-start | bytes 983048 | tf_op jit(solution)/shard_map/ppermute | solution.py:574
  21.8 0.3 shard_map.72
  22.1 6.8 %collective-permute-done.2.from_west = f32[160,512]{1,0:T(8,128)S(1)} collective-permute-done((f32[160,512]{1,0:T(8,128)S(1)}, f32[160,512]{1,0:T(8,128)S(1)}, u32[]{:S(2)}, u32[]{:S(2)}) %collective-permute-start.2) | collective-permute-done | bytes 327712 | tf_op jit(solution)/shard_map/ppermute | solution.py:574
  29.0 0.3 collective-permute-done.3.from_east
  29.2 0.0 copy-done.1
  29.2 5.1 %shard_map.73 = (f32[12,32,512]{2,1,0:T(8,128)}, f32[32,512]{1,0:T(8,128)}) custom-call(f32[4]{0:T(128)S(1)} %copy-done.4, f32[2,5,12,8,512]{4,3,2,1,0:T(8,128)S(1)} %copy-done.1, s32[32,512]{1,0:T(8,128)S(1)} %copy-done.2, s32[32,512]{1,0:T(8,128)S(1)} %copy-done.3, ...), custom_call_target="tpu_custom_call", output_to_operand_aliasing={{0}: (8, {}), {1}: (9, {})} | custom-call | tf_op jit(solution)/shard_map/pallas_call | solution.py:622
  (2 shorter events, 0.1 us)
Async XLA Ops:
  0.6 10.3 %copy-start.2 = (s32[32,512]{1,0:T(8,128)S(1)}, s32[32,512]{1,0:T(8,128)}, u32[]{:S(2)}) copy-start(s32[32,512]{1,0:T(8,128)} %sea.9) | copy-start | bytes 196612
  0.6 7.5 %copy-start = (f32[12,32,512]{2,1,0:T(8,128)S(1)}, f32[12,32,512]{2,1,0:T(8,128)}, u32[]{:S(2)}) copy-start(f32[12,32,512]{2,1,0:T(8,128)} %cot.7) | copy-start | bytes 2359300
  3.3 9.1 %copy-start.3 = (s32[32,512]{1,0:T(8,128)S(1)}, s32[32,512]{1,0:T(8,128)}, u32[]{:S(2)}) copy-start(s32[32,512]{1,0:T(8,128)} %layer.5) | copy-start | bytes 196612
  3.3 9.1 %copy-start.4 = (f32[4]{0:T(128)S(1)}, f32[4]{0:T(128)}, u32[]{:S(2)}) copy-start(f32[4]{0:T(128)} %gravities_in.1) | copy-start | bytes 52
  3.3 7.6 %collective-permute-start.1 = (f32[4,32,128]{2,1,0:T(8,128)}, f32[4,32,128]{2,1,0:T(8,128)S(1)}, u32[]{:S(2)}, u32[]{:S(2)}) collective-permute-start(f32[4,32,128]{2,1,0:T(8,128)} %shard_map.69), channel_id=1, source_target_pairs={{1,2},{5,6},{9,10},{13,14},{17,18},{21,22},{25,26},{29,30},{33,34}... | collective-permute-start | bytes 196616 | tf_op jit(solution)/shard_map/ppermute | solution.py:571
  8.0 2.9 %collective-permute-start = (f32[4,32,128]{2,1,0:T(8,128)}, f32[4,32,128]{2,1,0:T(8,128)S(1)}, u32[]{:S(2)}, u32[]{:S(2)}) collective-permute-start(f32[4,32,128]{2,1,0:T(8,128)} %shard_map.69), channel_id=1, source_target_pairs={{0,1},{2,3},{4,5},{6,7},{8,9},{10,11},{12,13},{14,15},{16,17},{18,... | collective-permute-start | bytes 196616 | tf_op jit(solution)/shard_map/ppermute | solution.py:571
  11.1 17.8 %collective-permute-start.2 = (f32[160,512]{1,0:T(8,128)S(1)}, f32[160,512]{1,0:T(8,128)S(1)}, u32[]{:S(2)}, u32[]{:S(2)}) collective-permute-start(f32[160,512]{1,0:T(8,128)S(1)} %get-tuple-element.16), channel_id=1, source_target_pairs={{0,4},{4,8},{8,12},{12,16},{16,20},{20,24},{24,28},{28,32},{32,36}... | collective-permute-start | bytes 983048 | tf_op jit(solution)/shard_map/ppermute | solution.py:574
  20.6 8.6 %copy-start.1 = (f32[2,5,12,8,512]{4,3,2,1,0:T(8,128)S(1)}, f32[2,5,12,8,512]{4,3,2,1,0:T(8,128)}, u32[]{:S(2)}) copy-start(f32[2,5,12,8,512]{4,3,2,1,0:T(8,128)} %get-tuple-element.13.own) | copy-start | bytes 5898244
  20.7 8.6 %collective-permute-start.3 = (f32[160,512]{1,0:T(8,128)S(1)}, f32[160,512]{1,0:T(8,128)S(1)}, u32[]{:S(2)}, u32[]{:S(2)}) collective-permute-start(f32[160,512]{1,0:T(8,128)S(1)} %get-tuple-element.19), channel_id=1, source_target_pairs={{0,252},{4,0},{8,4},{12,8},{16,12},{20,16},{24,20},{28,24},{32,28}... | collective-permute-start | bytes 983048 | tf_op jit(solution)/shard_map/ppermute | solution.py:574

commit v5 on v4

--- a/solution.py
+++ b/solution.py
@@ -65,14 +65,20 @@
 
 
 def strip_pack_kernel(states, cot, sea, strips, left, right, flags, sems):
-    pairs = [(sea, flags)]
-    for buf, cols in ((left, slice(0, 128)), (right, slice(COLS - 128, COLS))):
-        pairs.append((states.at[:, :, :, cols], buf.at[:N]))
-        pairs.append((cot.at[:, :, cols], buf.at[N]))
-    wait(start(pairs, sems))
+    copies = []
+    for n in range(N + 1):
+        source = cot if n == N else states.at[n]
+        pairs = [
+            (source.at[:, :, slice(0, 128)], left.at[n]),
+            (source.at[:, :, slice(COLS - 128, COLS)], right.at[n]),
+        ]
+        copies.append(start(pairs, sems.at[n]))
+    copies[N].extend(start([(sea, flags)], sems.at[N + 1]))
     lane = lax.broadcasted_iota(jnp.int32, (ROWS, 128), 1)
     for g in range(GROUPS):
         total = jnp.zeros((ROWS, 128), f32)
+        while copies and (N + 1 - len(copies)) * CH < g * 16 + 16:
+            wait(copies.pop(0))
         for k in range(16):
             q = g * 16 + k
             if q >= PLANES:
@@ -558,7 +564,7 @@
             pltpu.VMEM((N + 1, CH, ROWS, 128), f32),
             pltpu.VMEM((N + 1, CH, ROWS, 128), f32),
             pltpu.VMEM((ROWS, COLS), jnp.int32),
-            DMA((5,)),
+            DMA((N + 2, 2)),
         ],
         compiler_params=pltpu.CompilerParams(vmem_limit_bytes=60 << 20),
     )(saved_states, final_cotangent, sea_mask)

time: 34.5 us -> 34.5 us (level)
  no operation moved by 1% of the time
where the time goes in v5:
time: 34.5 us; the launch traced here: 34.3 us
  Pallas kernels  19.1 us (55%)
  starting transfers between devices  7.22 us (21%)
  waiting for transfers between devices  7.12 us (21%)
  between operations  0.77 us (2%)
    pallas_call x1, Pallas kernels, per_device(): pl.pallas_call(early_kernel, out_shape=outs + [shape((MESSAGE, COLS), f32...  8.23 us
    ppermute x2, waiting for transfers between devices, shift(): return lax.ppermute(x, 'lon', [(i, (i + by) % lons) for i in range(lons)])  7.11 us
    pallas_call x1, Pallas kernels, per_device(): pl.pallas_call(rim_kernel, out_shape=outs, in_specs=[ANY, VMEM, ANY, ANY,...  5.12 us
    ppermute x2, starting transfers between devices, swap(): return lax.ppermute(x, ('lon', 'lat'), pairs + [(b, a) for a, b in pairs])  4.82 us
    pallas_call x1, Pallas kernels, per_device(): pl.pallas_call(row_pack_kernel, out_shape=[shape((MESSAGE, COLS), f32)] *...  2.71 us
    pallas_call x1, Pallas kernels, per_device(): pl.pallas_call(strip_pack_kernel, out_shape=shape((GROUPS, ROWS, 128), f3...  2.57 us
    ppermute x2, starting transfers between devices, shift(): return lax.ppermute(x, 'lon', [(i, (i + by) % lons) for i in range(lons)])  2.4 us
  transfers between devices with their start and end apart: 4, of which 2 were waited for; matrix products, arithmetic and copies ran while one was open for 0% of the time, Pallas kernels for 33%

profile of v5, /device:TPU:1, one launch (start us, length us, event | category | flops | bytes accessed | tf_op | source)
XLA Modules:
  0.0 34.3 jit_solution(2864722574483465836)
XLA Ops:
  0.6 0.0 copy-start.2
  0.6 0.0 copy-start
  0.6 2.6 %shard_map.69 = f32[4,32,128]{2,1,0:T(8,128)} custom-call(f32[4,12,32,512]{3,2,1,0:T(8,128)} %states.7, f32[12,32,512]{2,1,0:T(8,128)} %cot.7, s32[32,512]{1,0:T(8,128)} %sea.9), custom_call_target="tpu_custom_call" | custom-call | tf_op jit(solution)/shard_map/pallas_call | solution.py:558
  3.2 0.0 copy-start.3
  3.2 0.0 copy-start.4
  3.3 4.7 %collective-permute-start.1 = (f32[4,32,128]{2,1,0:T(8,128)}, f32[4,32,128]{2,1,0:T(8,128)S(1)}, u32[]{:S(2)}, u32[]{:S(2)}) collective-permute-start(f32[4,32,128]{2,1,0:T(8,128)} %shard_map.69), channel_id=1, source_target_pairs={{1,2},{5,6},{9,10},{13,14},{17,18},{21,22},{25,26},{29,30},{33,34}... | collective-permute-start | bytes 196616 | tf_op jit(solution)/shard_map/ppermute | solution.py:577
  8.0 0.1 collective-permute-start
  8.1 0.0 copy-done
  8.1 2.7 %shard_map.68 = (f32[160,512]{1,0:T(8,128)S(1)}, f32[160,512]{1,0:T(8,128)S(1)}, f32[2,5,12,8,512]{4,3,2,1,0:T(8,128)}) custom-call(f32[4,12,32,512]{3,2,1,0:T(8,128)} %states.7, f32[12,32,512]{2,1,0:T(8,128)S(1)} %copy-done), custom_call_target="tpu_custom_call" | custom-call | tf_op jit(solution)/shard_map/pallas_call | solution.py:583
  10.9 0.0 collective-permute-done.1.middle
  10.9 0.0 collective-permute-done.pair
  10.9 0.0 copy-done.2
  10.9 0.2 shard_map.70
  11.1 1.3 %collective-permute-start.2 = (f32[160,512]{1,0:T(8,128)S(1)}, f32[160,512]{1,0:T(8,128)S(1)}, u32[]{:S(2)}, u32[]{:S(2)}) collective-permute-start(f32[160,512]{1,0:T(8,128)S(1)} %get-tuple-element.16), channel_id=1, source_target_pairs={{0,4},{4,8},{8,12},{12,16},{16,20},{20,24},{24,28},{28,32},{32,36}... | collective-permute-start | bytes 983048 | tf_op jit(solution)/shard_map/ppermute | solution.py:580
  12.4 0.0 copy-done.3
  12.4 0.0 copy-done.4
  12.4 8.2 %shard_map.71 = (f32[12,32,512]{2,1,0:T(8,128)}, f32[32,512]{1,0:T(8,128)}, f32[160,512]{1,0:T(8,128)S(1)}) custom-call(f32[4]{0:T(128)S(1)} %copy-done.4, f32[4,12,32,512]{3,2,1,0:T(8,128)} %states.7, f32[12,32,512]{2,1,0:T(8,128)S(1)} %copy-done, s32[32,512]{1,0:T(8,128)S(1)} %copy-done.2, ...), custom_call_target="tpu_custom_call", output_to_operand_aliasing={{2}: (7, {})} | custom-call | flops 160000000 | bytes 24000000 | tf_op jit(solution)/shard_map/pallas_call | solution.py:610
  20.6 0.0 copy-start.1
  20.6 1.1 %collective-permute-start.3 = (f32[160,512]{1,0:T(8,128)S(1)}, f32[160,512]{1,0:T(8,128)S(1)}, u32[]{:S(2)}, u32[]{:S(2)}) collective-permute-start(f32[160,512]{1,0:T(8,128)S(1)} %get-tuple-element.19), channel_id=1, source_target_pairs={{0,252},{4,0},{8,4},{12,8},{16,12},{20,16},{24,20},{28,24},{32,28}... | collective-permute-start | bytes 983048 | tf_op jit(solution)/shard_map/ppermute | solution.py:580
  21.7 0.3 shard_map.72
  22.1 6.8 %collective-permute-done.2.from_west = f32[160,512]{1,0:T(8,128)S(1)} collective-permute-done((f32[160,512]{1,0:T(8,128)S(1)}, f32[160,512]{1,0:T(8,128)S(1)}, u32[]{:S(2)}, u32[]{:S(2)}) %collective-permute-start.2) | collective-permute-done | bytes 327712 | tf_op jit(solution)/shard_map/ppermute | solution.py:580
  28.9 0.3 collective-permute-done.3.from_east
  29.2 0.0 copy-done.1
  29.2 5.1 %shard_map.73 = (f32[12,32,512]{2,1,0:T(8,128)}, f32[32,512]{1,0:T(8,128)}) custom-call(f32[4]{0:T(128)S(1)} %copy-done.4, f32[2,5,12,8,512]{4,3,2,1,0:T(8,128)S(1)} %copy-done.1, s32[32,512]{1,0:T(8,128)S(1)} %copy-done.2, s32[32,512]{1,0:T(8,128)S(1)} %copy-done.3, ...), custom_call_target="tpu_custom_call", output_to_operand_aliasing={{0}: (8, {}), {1}: (9, {})} | custom-call | tf_op jit(solution)/shard_map/pallas_call | solution.py:628
  (2 shorter events, 0.1 us)
Async XLA Ops:
  0.6 10.3 %copy-start.2 = (s32[32,512]{1,0:T(8,128)S(1)}, s32[32,512]{1,0:T(8,128)}, u32[]{:S(2)}) copy-start(s32[32,512]{1,0:T(8,128)} %sea.9) | copy-start | bytes 196612
  0.6 7.5 %copy-start = (f32[12,32,512]{2,1,0:T(8,128)S(1)}, f32[12,32,512]{2,1,0:T(8,128)}, u32[]{:S(2)}) copy-start(f32[12,32,512]{2,1,0:T(8,128)} %cot.7) | copy-start | bytes 2359300
  3.2 9.1 %copy-start.3 = (s32[32,512]{1,0:T(8,128)S(1)}, s32[32,512]{1,0:T(8,128)}, u32[]{:S(2)}) copy-start(s32[32,512]{1,0:T(8,128)} %layer.5) | copy-start | bytes 196612
  3.2 9.1 %copy-start.4 = (f32[4]{0:T(128)S(1)}, f32[4]{0:T(128)}, u32[]{:S(2)}) copy-start(f32[4]{0:T(128)} %gravities_in.1) | copy-start | bytes 52
  3.3 7.6 %collective-permute-start.1 = (f32[4,32,128]{2,1,0:T(8,128)}, f32[4,32,128]{2,1,0:T(8,128)S(1)}, u32[]{:S(2)}, u32[]{:S(2)}) collective-permute-start(f32[4,32,128]{2,1,0:T(8,128)} %shard_map.69), channel_id=1, source_target_pairs={{1,2},{5,6},{9,10},{13,14},{17,18},{21,22},{25,26},{29,30},{33,34}... | collective-permute-start | bytes 196616 | tf_op jit(solution)/shard_map/ppermute | solution.py:577
  8.0 2.9 %collective-permute-start = (f32[4,32,128]{2,1,0:T(8,128)}, f32[4,32,128]{2,1,0:T(8,128)S(1)}, u32[]{:S(2)}, u32[]{:S(2)}) collective-permute-start(f32[4,32,128]{2,1,0:T(8,128)} %shard_map.69), channel_id=1, source_target_pairs={{0,1},{2,3},{4,5},{6,7},{8,9},{10,11},{12,13},{14,15},{16,17},{18,... | collective-permute-start | bytes 196616 | tf_op jit(solution)/shard_map/ppermute | solution.py:577
  11.1 17.8 %collective-permute-start.2 = (f32[160,512]{1,0:T(8,128)S(1)}, f32[160,512]{1,0:T(8,128)S(1)}, u32[]{:S(2)}, u32[]{:S(2)}) collective-permute-start(f32[160,512]{1,0:T(8,128)S(1)} %get-tuple-element.16), channel_id=1, source_target_pairs={{0,4},{4,8},{8,12},{12,16},{16,20},{20,24},{24,28},{28,32},{32,36}... | collective-permute-start | bytes 983048 | tf_op jit(solution)/shard_map/ppermute | solution.py:580
  20.6 8.6 %copy-start.1 = (f32[2,5,12,8,512]{4,3,2,1,0:T(8,128)S(1)}, f32[2,5,12,8,512]{4,3,2,1,0:T(8,128)}, u32[]{:S(2)}) copy-start(f32[2,5,12,8,512]{4,3,2,1,0:T(8,128)} %get-tuple-element.13.own) | copy-start | bytes 5898244
  20.6 8.6 %collective-permute-start.3 = (f32[160,512]{1,0:T(8,128)S(1)}, f32[160,512]{1,0:T(8,128)S(1)}, u32[]{:S(2)}, u32[]{:S(2)}) collective-permute-start(f32[160,512]{1,0:T(8,128)S(1)} %get-tuple-element.19), channel_id=1, source_target_pairs={{0,252},{4,0},{8,4},{12,8},{16,12},{20,16},{24,20},{28,24},{32,28}... | collective-permute-start | bytes 983048 | tf_op jit(solution)/shard_map/ppermute | solution.py:580

commit v6 on v5

--- a/solution.py
+++ b/solution.py
@@ -451,6 +451,18 @@
             idx = jnp.concatenate([picked[j, 8 * r : 8 * r + 8, :] for j in range(W - 1)], axis=1)
             acc[r] = acc[r] + jnp.where(idx == level[:, :COLS], TIME_STEP * row(src, 0, 4 + r)[:, :COLS], 0.0)
 
+        if n == 0:
+            wait(back)
+            results = []
+            for e, start_row in enumerate((0, ROWS - 8)):
+                for r in range(4):
+                    total = acc[r]
+                    total = total + pltpu.roll(total, 4, 0)
+                    total = total + pltpu.roll(total, 2, 0)
+                    at = r if e == 0 else 4 + r
+                    tiles[e, CH, at : at + 1, :] = total[e : e + 1, :]
+                results += start([(tiles.at[e, CH], forcing.at[start_row : start_row + 8, :])], more.at[2 + e :])
+
         def one_row(r):
             c, p, q = row(src, 0, r), row(src, 1, r), row(src, 2, r)
             h, u, v = row(fields, 0, r), row(fields, 1, r), row(fields, 2, r)
@@ -503,26 +515,13 @@
 
         lax.fori_loop(0, 5 - i, rows_body, 0)
 
-    wait(back)
-    pairs = []
     for e, start_row in enumerate((0, ROWS - 8)):
         part = slice(0, 4) if e == 0 else slice(4, 8)
         for c in range(CH):
             for j in range(W - 1):
                 tiles[e, c, part, lanes(j)] = cur[c // L, j, pl.ds(32 + 2 * (c % L) + e, 4, stride=8), :]
-        pairs.append((tiles.at[e, :CH], out.at[:, start_row : start_row + 8, :]))
-    copies = start(pairs, more)
-    pairs = []
-    for e, start_row in enumerate((0, ROWS - 8)):
-        for r in range(4):
-            total = acc[r]
-            total = total + pltpu.roll(total, 4, 0)
-            total = total + pltpu.roll(total, 2, 0)
-            at = r if e == 0 else 4 + r
-            tiles[e, CH, at : at + 1, :] = total[e : e + 1, :]
-        pairs.append((tiles.at[e, CH], forcing.at[start_row : start_row + 8, :]))
-    copies = copies + start(pairs, more.at[2:])
-    wait(copies)
+        results += start([(tiles.at[e, :CH], out.at[:, start_row : start_row + 8, :])], more.at[e:])
+    wait(results)
 
 
 VMEM = pl.BlockSpec(memory_space=pltpu.VMEM)

time: 34.5 us -> 34.5 us (level)
  no operation moved by 1% of the time
where the time goes in v6:
time: 34.5 us; the launch traced here: 34.3 us
  Pallas kernels  19.1 us (55%)
  starting transfers between devices  7.22 us (21%)
  waiting for transfers between devices  7.12 us (21%)
  between operations  0.77 us (2%)
    pallas_call x1, Pallas kernels, per_device(): pl.pallas_call(early_kernel, out_shape=outs + [shape((MESSAGE, COLS), f32...  8.23 us
    ppermute x2, waiting for transfers between devices, shift(): return lax.ppermute(x, 'lon', [(i, (i + by) % lons) for i in range(lons)])  7.11 us
    pallas_call x1, Pallas kernels, per_device(): pl.pallas_call(rim_kernel, out_shape=outs, in_specs=[ANY, VMEM, ANY, ANY,...  5.1 us
    ppermute x2, starting transfers between devices, swap(): return lax.ppermute(x, ('lon', 'lat'), pairs + [(b, a) for a, b in pairs])  4.82 us
    pallas_call x1, Pallas kernels, per_device(): pl.pallas_call(row_pack_kernel, out_shape=[shape((MESSAGE, COLS), f32)] *...  2.71 us
    pallas_call x1, Pallas kernels, per_device(): pl.pallas_call(strip_pack_kernel, out_shape=shape((GROUPS, ROWS, 128), f3...  2.57 us
    ppermute x2, starting transfers between devices, shift(): return lax.ppermute(x, 'lon', [(i, (i + by) % lons) for i in range(lons)])  2.4 us
  transfers between devices with their start and end apart: 4, of which 2 were waited for; matrix products, arithmetic and copies ran while one was open for 0% of the time, Pallas kernels for 33%

profile of v6, /device:TPU:1, one launch (start us, length us, event | category | flops | bytes accessed | tf_op | source)
XLA Modules:
  0.0 34.3 jit_solution(5206239989064095947)
XLA Ops:
  0.6 0.0 copy-start.2
  0.6 0.0 copy-start
  0.6 2.6 %shard_map.69 = f32[4,32,128]{2,1,0:T(8,128)} custom-call(f32[4,12,32,512]{3,2,1,0:T(8,128)} %states.7, f32[12,32,512]{2,1,0:T(8,128)} %cot.7, s32[32,512]{1,0:T(8,128)} %sea.9), custom_call_target="tpu_custom_call" | custom-call | tf_op jit(solution)/shard_map/pallas_call | solution.py:557
  3.2 0.0 copy-start.3
  3.2 0.0 copy-start.4
  3.3 4.7 %collective-permute-start.1 = (f32[4,32,128]{2,1,0:T(8,128)}, f32[4,32,128]{2,1,0:T(8,128)S(1)}, u32[]{:S(2)}, u32[]{:S(2)}) collective-permute-start(f32[4,32,128]{2,1,0:T(8,128)} %shard_map.69), channel_id=1, source_target_pairs={{1,2},{5,6},{9,10},{13,14},{17,18},{21,22},{25,26},{29,30},{33,34}... | collective-permute-start | bytes 196616 | tf_op jit(solution)/shard_map/ppermute | solution.py:576
  8.0 0.1 collective-permute-start
  8.1 0.0 copy-done
  8.1 2.7 %shard_map.68 = (f32[160,512]{1,0:T(8,128)S(1)}, f32[160,512]{1,0:T(8,128)S(1)}, f32[2,5,12,8,512]{4,3,2,1,0:T(8,128)}) custom-call(f32[4,12,32,512]{3,2,1,0:T(8,128)} %states.7, f32[12,32,512]{2,1,0:T(8,128)S(1)} %copy-done), custom_call_target="tpu_custom_call" | custom-call | tf_op jit(solution)/shard_map/pallas_call | solution.py:582
  10.9 0.0 collective-permute-done.1.middle
  10.9 0.0 collective-permute-done.pair
  10.9 0.0 copy-done.2
  10.9 0.2 shard_map.70
  11.1 1.3 %collective-permute-start.2 = (f32[160,512]{1,0:T(8,128)S(1)}, f32[160,512]{1,0:T(8,128)S(1)}, u32[]{:S(2)}, u32[]{:S(2)}) collective-permute-start(f32[160,512]{1,0:T(8,128)S(1)} %get-tuple-element.16), channel_id=1, source_target_pairs={{0,4},{4,8},{8,12},{12,16},{16,20},{20,24},{24,28},{28,32},{32,36}... | collective-permute-start | bytes 983048 | tf_op jit(solution)/shard_map/ppermute | solution.py:579
  12.4 0.0 copy-done.3
  12.4 0.0 copy-done.4
  12.4 8.2 %shard_map.71 = (f32[12,32,512]{2,1,0:T(8,128)}, f32[32,512]{1,0:T(8,128)}, f32[160,512]{1,0:T(8,128)S(1)}) custom-call(f32[4]{0:T(128)S(1)} %copy-done.4, f32[4,12,32,512]{3,2,1,0:T(8,128)} %states.7, f32[12,32,512]{2,1,0:T(8,128)S(1)} %copy-done, s32[32,512]{1,0:T(8,128)S(1)} %copy-done.2, ...), custom_call_target="tpu_custom_call", output_to_operand_aliasing={{2}: (7, {})} | custom-call | flops 160000000 | bytes 24000000 | tf_op jit(solution)/shard_map/pallas_call | solution.py:609
  20.6 0.0 copy-start.1
  20.6 1.1 %collective-permute-start.3 = (f32[160,512]{1,0:T(8,128)S(1)}, f32[160,512]{1,0:T(8,128)S(1)}, u32[]{:S(2)}, u32[]{:S(2)}) collective-permute-start(f32[160,512]{1,0:T(8,128)S(1)} %get-tuple-element.19), channel_id=1, source_target_pairs={{0,252},{4,0},{8,4},{12,8},{16,12},{20,16},{24,20},{28,24},{32,28}... | collective-permute-start | bytes 983048 | tf_op jit(solution)/shard_map/ppermute | solution.py:579
  21.7 0.3 shard_map.72
  22.1 6.8 %collective-permute-done.2.from_west = f32[160,512]{1,0:T(8,128)S(1)} collective-permute-done((f32[160,512]{1,0:T(8,128)S(1)}, f32[160,512]{1,0:T(8,128)S(1)}, u32[]{:S(2)}, u32[]{:S(2)}) %collective-permute-start.2) | collective-permute-done | bytes 327712 | tf_op jit(solution)/shard_map/ppermute | solution.py:579
  28.9 0.3 collective-permute-done.3.from_east
  29.2 0.0 copy-done.1
  29.2 5.1 %shard_map.73 = (f32[12,32,512]{2,1,0:T(8,128)}, f32[32,512]{1,0:T(8,128)}) custom-call(f32[4]{0:T(128)S(1)} %copy-done.4, f32[2,5,12,8,512]{4,3,2,1,0:T(8,128)S(1)} %copy-done.1, s32[32,512]{1,0:T(8,128)S(1)} %copy-done.2, s32[32,512]{1,0:T(8,128)S(1)} %copy-done.3, ...), custom_call_target="tpu_custom_call", output_to_operand_aliasing={{0}: (8, {}), {1}: (9, {})} | custom-call | tf_op jit(solution)/shard_map/pallas_call | solution.py:627
  (2 shorter events, 0.1 us)
Async XLA Ops:
  0.6 10.3 %copy-start.2 = (s32[32,512]{1,0:T(8,128)S(1)}, s32[32,512]{1,0:T(8,128)}, u32[]{:S(2)}) copy-start(s32[32,512]{1,0:T(8,128)} %sea.9) | copy-start | bytes 196612
  0.6 7.5 %copy-start = (f32[12,32,512]{2,1,0:T(8,128)S(1)}, f32[12,32,512]{2,1,0:T(8,128)}, u32[]{:S(2)}) copy-start(f32[12,32,512]{2,1,0:T(8,128)} %cot.7) | copy-start | bytes 2359300
  3.2 9.1 %copy-start.3 = (s32[32,512]{1,0:T(8,128)S(1)}, s32[32,512]{1,0:T(8,128)}, u32[]{:S(2)}) copy-start(s32[32,512]{1,0:T(8,128)} %layer.5) | copy-start | bytes 196612
  3.2 9.1 %copy-start.4 = (f32[4]{0:T(128)S(1)}, f32[4]{0:T(128)}, u32[]{:S(2)}) copy-start(f32[4]{0:T(128)} %gravities_in.1) | copy-start | bytes 52
  3.3 7.6 %collective-permute-start.1 = (f32[4,32,128]{2,1,0:T(8,128)}, f32[4,32,128]{2,1,0:T(8,128)S(1)}, u32[]{:S(2)}, u32[]{:S(2)}) collective-permute-start(f32[4,32,128]{2,1,0:T(8,128)} %shard_map.69), channel_id=1, source_target_pairs={{1,2},{5,6},{9,10},{13,14},{17,18},{21,22},{25,26},{29,30},{33,34}... | collective-permute-start | bytes 196616 | tf_op jit(solution)/shard_map/ppermute | solution.py:576
  8.0 2.9 %collective-permute-start = (f32[4,32,128]{2,1,0:T(8,128)}, f32[4,32,128]{2,1,0:T(8,128)S(1)}, u32[]{:S(2)}, u32[]{:S(2)}) collective-permute-start(f32[4,32,128]{2,1,0:T(8,128)} %shard_map.69), channel_id=1, source_target_pairs={{0,1},{2,3},{4,5},{6,7},{8,9},{10,11},{12,13},{14,15},{16,17},{18,... | collective-permute-start | bytes 196616 | tf_op jit(solution)/shard_map/ppermute | solution.py:576
  11.1 17.8 %collective-permute-start.2 = (f32[160,512]{1,0:T(8,128)S(1)}, f32[160,512]{1,0:T(8,128)S(1)}, u32[]{:S(2)}, u32[]{:S(2)}) collective-permute-start(f32[160,512]{1,0:T(8,128)S(1)} %get-tuple-element.16), channel_id=1, source_target_pairs={{0,4},{4,8},{8,12},{12,16},{16,20},{20,24},{24,28},{28,32},{32,36}... | collective-permute-start | bytes 983048 | tf_op jit(solution)/shard_map/ppermute | solution.py:579
  20.6 8.6 %copy-start.1 = (f32[2,5,12,8,512]{4,3,2,1,0:T(8,128)S(1)}, f32[2,5,12,8,512]{4,3,2,1,0:T(8,128)}, u32[]{:S(2)}) copy-start(f32[2,5,12,8,512]{4,3,2,1,0:T(8,128)} %get-tuple-element.13.own) | copy-start | bytes 5898244
  20.6 8.6 %collective-permute-start.3 = (f32[160,512]{1,0:T(8,128)S(1)}, f32[160,512]{1,0:T(8,128)S(1)}, u32[]{:S(2)}, u32[]{:S(2)}) collective-permute-start(f32[160,512]{1,0:T(8,128)S(1)} %get-tuple-element.19), channel_id=1, source_target_pairs={{0,252},{4,0},{8,4},{12,8},{16,12},{20,16},{24,20},{28,24},{32,28}... | collective-permute-start | bytes 983048 | tf_op jit(solution)/shard_map/ppermute | solution.py:579
